TPU v7x, 128 devices: a whole 4x4x4 slice. The times are simulated.
128 devices in a mesh: row: 8 (over y, core), col: 16 (over x, z).
Axes of the slice: x: 4, y: 4, z: 4, core: 2. Of those that a mesh axis runs over, the one named last changes fastest.
Arguments:
- sigma_ss: bfloat16 [8192, 8192], P('col', 'row')
- l_cs: bfloat16 [6144, 8192], P('row', 'col'), may hold values from -4 to 4
- g_cc: bfloat16 [6144, 6144], P('row', 'col')
- pattern: int32 [16, 64], P(None, 'col'), may hold values 0 or 1
- sup_sizes: int32 [16], replicated, may hold values from 1 to 4, 48 in all
- owner: int32 [6144], P(('row', 'col')), may hold values from 0 to 6143, each once
Outputs:
- sel_cs: float32 [6144, 8192], P('row', 'col')
- log_var: float32 [6144], P(('row', 'col'))
Inputs may be any that keep to these rules, and one draw needn't show every extreme that they name: `sup_sizes`: each child supernode holds between 1 and 4 blocks, and the sizes sum to 48. `owner`: each latent value of the child appears once.
All inputs are finite; a program needn't handle non-finite values. No bound on the sum of `pattern` on one device may be relied on, other than what follows from the above.
Results may differ from a plain program's by a relative error of at most 0.002.
The roundings to bfloat16 on the way count: a program that leaves them out, or rounds other values in their place, can miss the bound.
Values may be sent and summed in bfloat16 or wider, within the bound.
A program may use at most 128 MiB of HBM per device.

v0:
```python
import jax
import jax.numpy as jnp
from jax import lax
from jax.sharding import PartitionSpec as P

BLK = 128
NSUP = 16


def per_device(sigma_ss, l_cs, g_cc, pattern, sup_sizes, owner):
    local_rows = l_cs.shape[0]
    row_start = lax.axis_index("row") * local_rows
    row_ends = jnp.cumsum(sup_sizes) * BLK
    child_rows = row_start + jnp.arange(local_rows, dtype=jnp.int32)
    supernode = jnp.sum((child_rows[:, None] >= row_ends[None, :]).astype(jnp.int32), axis=1)
    one_hot = (supernode[:, None] == jnp.arange(NSUP, dtype=jnp.int32)[None, :]).astype(jnp.float32)
    block_mask = jnp.dot(one_hot, pattern.astype(jnp.float32), precision=lax.Precision.HIGHEST)
    full_mask = jnp.repeat(block_mask, BLK, axis=1)
    masked = (l_cs.astype(jnp.float32) * full_mask).astype(jnp.bfloat16)
    factor_rows = lax.all_gather(g_cc, "col", axis=1, tiled=True)
    child_total = factor_rows.shape[1]
    columns = factor_rows
    zeta = lax.psum_scatter(
        lax.dot_general(
            columns, masked, (((0,), (0,)), ((), ())), preferred_element_type=jnp.float32
        ),
        "row",
        scatter_dimension=0,
        tiled=True,
    ).astype(jnp.bfloat16)
    sep_rows = lax.all_gather(sigma_ss, "row", axis=1, tiled=True)
    columns = sep_rows
    coupling = -lax.dot_general(
        lax.all_gather(zeta, "col", axis=1, tiled=True),
        columns,
        (((1,), (1,)), ((), ())),
        preferred_element_type=jnp.float32,
    )
    sel_cs = full_mask * coupling
    g_wide = g_cc.astype(jnp.float32)
    factor_part = jnp.sum(g_wide * g_wide, axis=0)
    cross_part = jnp.sum(coupling * zeta.astype(jnp.float32), axis=1)
    zero_vector = jnp.zeros((child_total,), jnp.float32)
    factor_vector = lax.dynamic_update_slice(
        zero_vector, factor_part, (lax.axis_index("col") * g_cc.shape[1],)
    )
    cross_vector = lax.dynamic_update_slice(zero_vector, -cross_part, (row_start,))
    variance = lax.psum(factor_vector + cross_vector, ("row", "col"))
    log_all = jnp.log(variance)
    positions = jnp.arange(child_total, dtype=jnp.int32)
    log_var = jnp.sum(
        jnp.where(owner[:, None] == positions[None, :], log_all[None, :], 0.0), axis=1
    )
    return (sel_cs, log_var)


def solution(mesh):
    in_specs = (
        P("col", "row"),
        P("row", "col"),
        P("row", "col"),
        P(None, "col"),
        P(),
        P(("row", "col")),
    )
    out_specs = (P("row", "col"), P(("row", "col")))
    return jax.shard_map(
        per_device, mesh=mesh, in_specs=in_specs, out_specs=out_specs, check_vma=False
    )
```

profile of v0, /device:TPU:1, one launch (start us, length us, event | category | flops | bytes accessed | tf_op | source)
XLA Modules:
  0.0 411.6 jit_solution(17284296094048209147)
XLA Ops:
  7.2 0.0 copy-start.2
  7.2 0.0 all-gather.4.cloned.1.call-start
  7.2 0.7 all-gather.4.cloned.1.call-update
  7.9 0.0 reduce-scatter.2.cloned.1.call-start
  8.0 0.7 copy.14
  8.7 1.4 copy.15
  10.1 0.1 multiply_reduce_fusion.2
  10.3 0.1 convert_reduce_fusion
  10.3 0.0 copy-done.2
  10.4 0.4 fusion.1
  10.7 0.2 fusion
  10.9 85.4 %all-gather.4.cloned.1.call-done = bf16[768,6144]{1,0:T(8,128)(2,1)} async-done(((bf16[768,384]{1,0:T(8,128)(2,1)}), bf16[768,6144]{1,0:T(8,128)(2,1)}) %all-gather.4.cloned.1.call-update) | async-done | bytes 9437200 | tf_op jit(solution)/shard_map/all_gather | solution.py:20
  96.3 11.7 %convolution_bitcast_fusion = f32[6144,512]{0,1:T(8,128)} fusion(bf16[768,512]{0,1:T(8,128)(2,1)S(1)} %fusion, bf16[768,6144]{1,0:T(8,128)(2,1)} %all-gather.4.cloned.1.call-done), kind=kOutput, calls=%fused_computation | convolution fusion | flops 4831838208 | bytes 22806528 | tf_op jit(solution)/shard_map/dot_general | solution.py:24
  108.0 0.0 reduce-scatter.2.cloned.1.call-update
  108.0 0.0 all-gather.8.cloned.1.call-start
  108.1 0.7 all-gather.8.cloned.1.call-update
  108.8 0.0 copy-start
  108.8 0.0 all-gather.6.cloned.1.call-start
  108.8 71.3 %reduce-scatter.2.cloned.1.call-done = f32[768,512]{0,1:T(8,128)} async-done(((f32[6144,512]{0,1:T(8,128)}), f32[768,512]{0,1:T(8,128)}) %reduce-scatter.2.cloned.1.call-update) | async-done | bytes 1572880 | tf_op jit(solution)/shard_map/reduce_scatter | solution.py:23
  180.1 2.4 convert_element_type.26
  182.5 0.0 all-gather.6.cloned.1.call-update
  182.5 0.0 copy-done
  182.5 0.2 multiply_reduce_fusion.1
  182.7 0.3 dynamic_update_slice.8
  183.0 49.1 %all-gather.8.cloned.1.call-done = bf16[512,8192]{1,0:T(8,128)(2,1)} async-done(((bf16[512,1024]{1,0:T(8,128)(2,1)}), bf16[512,8192]{1,0:T(8,128)(2,1)}) %all-gather.8.cloned.1.call-update) | async-done | bytes 8388624 | tf_op jit(solution)/shard_map/all_gather | solution.py:31
  232.1 92.6 %all-gather.6.cloned.1.call-done = bf16[768,8192]{0,1:T(8,128)(2,1)} async-done(((bf16[768,512]{0,1:T(8,128)(2,1)}), bf16[768,8192]{0,1:T(8,128)(2,1)}) %all-gather.6.cloned.1.call-update) | async-done | bytes 12582928 | tf_op jit(solution)/shard_map/all_gather | solution.py:34
  324.7 12.9 %multiply_reduce_fusion = (f32[768]{0:T(1024)S(1)}, f32[768,512]{0,1:T(8,128)S(1)}) fusion(bf16[768,512]{0,1:T(8,128)(2,1)} %convert_element_type.26, f32[768,4]{0,1:T(4,128)S(1)} %fusion.1, bf16[512,8192]{1,0:T(8,128)(2,1)} %all-gather.8.cloned.1.call-done, bf16[768,8192]{0,1:T(8,128)(2,1)} %all-gather.6.cloned.1.call-done), kind=kOutput, calls=%fused_computation.4 | convolution fusion | flops 6444416000 | bytes 23346176 | tf_op jit(solution)/shard_map/dot_general | solution.py:33
  337.6 0.2 add_dynamic-update-slice_fusion
  337.8 64.8 %psum.7 = f32[6144]{0:T(1024)S(1)} all-reduce(f32[6144]{0:T(1024)S(1)} %add_dynamic-update-slice_fusion), channel_id=1, replica_groups=mesh['row'=8,'col'=16] {'row','col'}, use_global_device_ids=true, to_apply=%region_5.6 | all-reduce | flops 6144 | bytes 49152 | tf_op jit(solution)/shard_map/psum | solution.py:48
  402.6 0.0 copy-start.1
  402.6 1.6 copy.16
  404.3 0.8 select_reduce_fusion
  (5 shorter events, 0.1 us)
Async XLA Ops:
  7.2 3.2 copy-start.2
  7.2 89.1 %all-gather.4.cloned.1.call-start = ((), (), s32[]{:S(2)}) async-start(), calls=%async_computation.1 | async-start | bytes 10027008 | tf_op jit(solution)/shard_map/all_gather | solution.py:20
  7.9 172.2 %reduce-scatter.2.cloned.1.call-start = ((), (), s32[]{:S(2)}) async-start(), calls=%async_computation.2 | async-start | bytes 14155776 | tf_op jit(solution)/shard_map/reduce_scatter | solution.py:23
  108.0 124.1 %all-gather.8.cloned.1.call-start = ((), (), s32[]{:S(2)}) async-start(), calls=%async_computation.4 | async-start | bytes 9437184 | tf_op jit(solution)/shard_map/all_gather | solution.py:31
  108.8 73.8 %copy-start = (bf16[768,384]{1,0:T(8,128)(2,1)S(1)}, bf16[768,384]{1,0:T(8,128)(2,1)}, u32[]{:S(2)}) copy-start(bf16[768,384]{1,0:T(8,128)(2,1)} %param.8) | copy-start | bytes 1769476
  108.8 215.9 %all-gather.6.cloned.1.call-start = ((), (), s32[]{:S(2)}) async-start(), calls=%async_computation.3 | async-start | bytes 13369344 | tf_op jit(solution)/shard_map/all_gather | solution.py:34
  402.6 1.6 copy-start.1
Sparse Core Ops, SparseCore 0:
  10.1 86.1 all-gather.3
  108.1 71.9 reduce-scatter.1
  181.8 50.2 all-gather.7
  234.7 89.9 all-gather.5
where the time goes:
time: 412 us
  waiting for transfers between devices  300 us (73%)
  blocking collectives  64.8 us (16%)
  matrix products  24.9 us (6%)
  between operations  13.9 us (3%)
    all_gather x1, waiting for transfers between devices, per_device(): lax.all_gather(zeta, 'col', axis=1, tiled=True)  92.6 us
    all_gather x1, waiting for transfers between devices, per_device(): factor_rows = lax.all_gather(g_cc, 'col', axis=1, tiled=True)  85.4 us
    reduce_scatter x1, waiting for transfers between devices, per_device(): lax.psum_scatter(lax.dot_general(columns, masked, (((0,), (0,)), ((), ())...  71.3 us
    psum x1, blocking collectives, per_device(): variance = lax.psum(factor_vector + cross_vector, ('row', 'col'))  64.8 us
    all_gather x1, waiting for transfers between devices, per_device(): sep_rows = lax.all_gather(sigma_ss, 'row', axis=1, tiled=True)  49.1 us
    dot_general x1, matrix products, per_device(): lax.dot_general(lax.all_gather(zeta, 'col', axis=1, tiled=True), columns,...  12.9 us
    dot_general x1, matrix products, per_device(): lax.dot_general(columns, masked, (((0,), (0,)), ((), ())), preferred_elem...  11.7 us
  transfers between devices with their start and end apart: 4, of which 4 were waited for; matrix products, arithmetic and copies ran while one was open for 1% of the time, Pallas kernels for 0%

commit v1 on v0

v1 whole, which is shorter than its diff:
```python
import jax
import jax.numpy as jnp
from jax import lax
from jax.experimental import pallas as pl
from jax.experimental.pallas import tpu as pltpu
from jax.sharding import PartitionSpec as P

BLK = 128
NSUP = 16
MESH = pl.DeviceIdType.MESH
F32 = jnp.float32
BF16 = jnp.bfloat16
NQ = 4
FAR_ORDER = (2, 1, 3)


def kernel(
    gt_ref, masked_ref, sigma_ref, fac_ref,
    out_ref, fout_ref, cout_ref,
    gbuf, mbuf, sbuf, acc, far, near, zc, pbuf, rz, cross, fa, fb, ca, cb,
    local_sem, ga_send, ga_recv, gg_send, gg_recv,
    m_send, m_recv, m_sib_send, m_sib_recv,
    sa_send, sa_recv, s_send, s_recv, s_sib_send, s_sib_recv,
    y_send, y_recv, x_send, x_recv, z_send, z_recv,
    fr_send, fr_recv, fc_send, fc_recv, cr_send, cr_recv, cc_send, cc_recv,
):
    r = lax.axis_index("row")
    c = lax.axis_index("col")
    y, i = r // 2, r % 2
    x, z = c // 4, c % 4
    sib = 2 * y + 1 - i
    t = z // 2
    same = i == t
    other = i != t

    def at_x(d):
        return lax.rem(x + d, 4)

    def at_y(d):
        return lax.rem(y + d, 4)

    def at_z(d):
        return lax.rem(z + d, 4)

    def remote(src, dst, send, recv, row, col):
        return pltpu.make_async_remote_copy(
            src_ref=src, dst_ref=dst, send_sem=send, recv_sem=recv,
            device_id=(row, col), device_id_type=MESH,
        )

    def arrived(dst, recv):
        pltpu.make_async_copy(dst, dst, recv).wait()

    pending = []

    def send(*args):
        copy = remote(*args)
        copy.start()
        pending.append(copy)

    barrier = pltpu.get_barrier_semaphore()
    partners = [(r, lax.rem(c + d, 16)) for d in range(1, 16)]
    partners += [(lax.rem(r + d, 8), c) for d in range(1, 8)]
    partners += [(sib, 4 * at_x(d) + z) for d in range(1, 4)]
    partners += [(sib, 4 * x + at_z(d)) for d in range(1, 4)]
    for partner in partners:
        pl.semaphore_signal(barrier, inc=1, device_id=partner, device_id_type=MESH)
    pl.semaphore_wait(barrier, len(partners))

    def factor_dst():
        return gbuf.at[lax.rem(z, 2), x, i]

    def factor_copies(rel):
        copies = []
        for d in range(0 if rel else 1, 4):
            copies.append(remote(
                gt_ref.at[at_x(d)], factor_dst(), ga_send.at[d], ga_recv.at[d, rel],
                2 * y + t, 4 * at_x(d) + z,
            ))
        return copies

    @pl.when(same)
    def _():
        pltpu.make_async_copy(gt_ref.at[x], factor_dst(), local_sem.at[0]).start()
        for copy in factor_copies(0):
            copy.start()

    @pl.when(other)
    def _():
        for copy in factor_copies(1):
            copy.start()

    def sigma_copy(l):
        return remote(
            sigma_ref.at[l], sbuf.at[y, z],
            sa_send.at[l], sa_recv.at[lax.rem(z, 2)], 2 * y + t, 4 * x + 2 * i + l,
        )

    def sigma_own():
        return pltpu.make_async_copy(sigma_ref.at[lax.rem(z, 2)], sbuf.at[y, z], local_sem.at[1])

    def sigma_other():
        l = 1 - lax.rem(z, 2)
        return remote(
            sigma_ref.at[l], sbuf.at[y, z],
            sa_send.at[l], sa_recv.at[lax.rem(z, 2)], 2 * y + t, 4 * x + 2 * i + l,
        )

    @pl.when(same)
    def _():
        sigma_own().start()
        sigma_other().start()

    @pl.when(other)
    def _():
        sigma_copy(0).start()
        sigma_copy(1).start()

    def ring_first(src, slot, snd, rcv, right, left, me):
        send(src(0), slot(me, 0), snd.at[0], rcv.at[0], *right)
        send(src(1), slot(me, 1), snd.at[2], rcv.at[2], *left)
        send(src(1), slot(me, 1), snd.at[1], rcv.at[1], *right)
        send(src(0), slot(me, 0), snd.at[3], rcv.at[3], *left)

    def ring_forward(slot, snd, rcv, right, left, at):
        arrived(slot(at(3), 0), rcv.at[0])
        send(slot(at(3), 0), slot(at(3), 0), snd.at[4], rcv.at[4], *right)
        arrived(slot(at(1), 1), rcv.at[2])
        send(slot(at(1), 1), slot(at(1), 1), snd.at[5], rcv.at[5], *left)

    def ring_rest(slot, rcv, at):
        arrived(slot(at(3), 1), rcv.at[1])
        arrived(slot(at(1), 0), rcv.at[3])

    def ring_far(slot, rcv, at):
        arrived(slot(at(2), 0), rcv.at[4])
        arrived(slot(at(2), 1), rcv.at[5])

    x_right, x_left = (r, 4 * at_x(1) + z), (r, 4 * at_x(3) + z)
    y_right, y_left = (2 * at_y(1) + i, c), (2 * at_y(3) + i, c)

    def m_slot(place, half):
        return mbuf.at[i, place, half]

    def m_share(n, place):
        send(mbuf.at[i, place], mbuf.at[i, place], m_sib_send.at[n], m_sib_recv.at[n], sib, c)

    def s_slot(place, half):
        return sbuf.at[place, 2 * i + half]

    def s_share(n, place):
        block = sbuf.at[place, pl.ds(2 * i, 2)]
        send(block, block, s_sib_send.at[n], s_sib_recv.at[n], sib, c)

    ring_first(lambda h: masked_ref.at[h], m_slot, m_send, m_recv, x_right, x_left, x)
    send(masked_ref, mbuf.at[i, x], m_sib_send.at[0], m_sib_recv.at[0], sib, c)
    own_masked = pltpu.make_async_copy(masked_ref, mbuf.at[i, x], local_sem.at[2])
    own_masked.start()

    fa[r] = fac_ref[...]
    for d in range(1, 8):
        send(fac_ref, fa.at[r], fr_send.at[d], fr_recv.at[d], lax.rem(r + d, 8), c)

    @pl.when(same)
    def _():
        sigma_own().wait()
        m = 1 - lax.rem(z, 2)
        arrived(sbuf.at[y, 2 * i + m], sa_recv.at[m])

    @pl.when(other)
    def _():
        arrived(sbuf.at[y, 2 * i], sa_recv.at[0])
        arrived(sbuf.at[y, 2 * i + 1], sa_recv.at[1])

    ring_first(lambda h: s_slot(y, h), s_slot, s_send, s_recv, y_right, y_left, y)
    s_share(0, y)

    def spread_copies():
        slot = gbuf.at[lax.rem(z, 2)]
        return [
            remote(slot, slot, gg_send.at[d], gg_recv.at[lax.rem(z, 2)], r, 4 * x + at_z(d))
            for d in FAR_ORDER
        ]

    @pl.when(same)
    def _():
        pltpu.make_async_copy(gt_ref.at[x], factor_dst(), local_sem.at[0]).wait()
        for d in range(4):
            for rel in range(2):
                if d or rel:
                    src_core = 1 - i if rel else i
                    arrived(gbuf.at[lax.rem(z, 2), at_x(4 - d), src_core], ga_recv.at[d, rel])
        for copy in spread_copies():
            copy.start()

    ring_forward(m_slot, m_send, m_recv, x_right, x_left, at_x)
    ring_rest(m_slot, m_recv, at_x)
    m_share(1, at_x(3))
    m_share(2, at_x(1))
    ring_forward(s_slot, s_send, s_recv, y_right, y_left, at_y)
    ring_rest(s_slot, s_recv, at_y)
    s_share(1, at_y(3))
    s_share(2, at_y(1))

    for d in range(1, 8):
        arrived(fa.at[lax.rem(r + 8 - d, 8)], fr_recv.at[d])
    fb[c] = jnp.sum(fa[...], axis=0)
    for d in range(1, 16):
        send(fb.at[c], fb.at[c], fc_send.at[d], fc_recv.at[d], r, lax.rem(c + d, 16))

    ring_far(m_slot, m_recv, at_x)
    m_share(3, at_x(2))
    own_masked.wait()
    for zl in range(2):
        @pl.when(z != 2 * i + zl)
        def _():
            arrived(gbuf.at[zl], gg_recv.at[zl])
    for n, d in enumerate((0, 3, 1, 2)):
        arrived(mbuf.at[1 - i, at_x(d)], m_sib_recv.at[n])

    def zeta_part(q):
        zl, half = q // 2, q % 2
        g0 = gbuf[zl, :, 0, half].reshape(192, 768)
        g1 = gbuf[zl, :, 1, half].reshape(192, 768)

        def step(k, carry):
            total = jnp.dot(g0, mbuf[0, k].reshape(768, 512), preferred_element_type=F32)
            total += jnp.dot(g1, mbuf[1, k].reshape(768, 512), preferred_element_type=F32)
            acc[q, :, k] = total.reshape(4, 48, 512)
            return carry

        lax.fori_loop(0, 4, step, 0)

    low, high = pl.ds(0, 2), pl.ds(2, 2)

    def y_far(q):
        send(acc.at[q, at_y(2), low], far.at[q, 0], y_send.at[q, 0], y_recv.at[q, 0], *y_right)
        send(acc.at[q, at_y(2), high], far.at[q, 1], y_send.at[q, 1], y_recv.at[q, 1], *y_left)

    def y_direct(q):
        send(acc.at[q, at_y(1), high], near.at[q, 0, high], y_send.at[q, 2], y_recv.at[q, 2], *y_right)
        send(acc.at[q, at_y(3), low], near.at[q, 1, low], y_send.at[q, 3], y_recv.at[q, 3], *y_left)

    def y_combined(q):
        arrived(far.at[q, 0], y_recv.at[q, 0])
        acc[q, at_y(1), 0:2] += far[q, 0]
        send(acc.at[q, at_y(1), low], near.at[q, 0, low], y_send.at[q, 4], y_recv.at[q, 4], *y_right)
        arrived(far.at[q, 1], y_recv.at[q, 1])
        acc[q, at_y(3), 2:4] += far[q, 1]
        send(acc.at[q, at_y(3), high], near.at[q, 1, high], y_send.at[q, 5], y_recv.at[q, 5], *y_left)

    def zeta_done(q):
        arrived(near.at[q, 0, high], y_recv.at[q, 2])
        arrived(near.at[q, 1, low], y_recv.at[q, 3])
        arrived(near.at[q, 0, low], y_recv.at[q, 4])
        arrived(near.at[q, 1, high], y_recv.at[q, 5])
        zc[q, :, x] = (acc[q, y] + near[q, 0] + near[q, 1]).astype(BF16)
        for d in FAR_ORDER:
            send(zc.at[q, :, x], zc.at[q, :, x], x_send.at[q, d - 1], x_recv.at[q, d - 1], r, 4 * at_x(d) + z)

    def product(q, zt):
        total = None
        for k in range(4):
            part = lax.dot_general(
                zc[q, k].reshape(192, 512), sbuf[k, zt],
                (((1,), (1,)), ((), ())), preferred_element_type=F32,
            )
            total = part if total is None else total + part
        return total

    def coupling_part(q):
        for d in range(1, 4):
            arrived(zc.at[q, :, at_x(4 - d)], x_recv.at[q, d - 1])
        for d in FAR_ORDER:
            pbuf[q, d - 1] = product(q, at_z(d)).astype(BF16)
            send(pbuf.at[q, d - 1], rz.at[q, d - 1], z_send.at[q, d - 1], z_recv.at[q, d - 1], r, 4 * x + at_z(d))
        out_ref[q // 2, :, q % 2] = product(q, z).reshape(4, 48, 512)

    def coupling_done(q):
        zl, half = q // 2, q % 2
        for d in range(3):
            arrived(rz.at[q, d], z_recv.at[q, d])
        total = out_ref[zl, :, half].reshape(192, 512)
        total += rz[q, 0].astype(F32) + rz[q, 1].astype(F32) + rz[q, 2].astype(F32)
        total = -total
        out_ref[zl, :, half] = total.reshape(4, 48, 512)
        terms = total * zc[q, x].reshape(192, 512).astype(F32)
        terms = terms[:, 0:128] + terms[:, 128:256] + terms[:, 256:384] + terms[:, 384:512]
        cross[zl, :, half] = terms.reshape(4, 48, 128)

    zeta_part(0)
    y_far(0)
    y_direct(0)
    zeta_part(1)
    y_far(1)
    ring_far(s_slot, s_recv, at_y)
    s_share(3, at_y(2))
    y_combined(0)
    y_direct(1)
    zeta_part(2)
    y_far(2)
    y_combined(1)
    y_direct(2)
    zeta_part(3)
    zeta_done(0)
    y_far(3)
    y_combined(2)
    y_direct(3)
    for n, d in enumerate((0, 3, 1, 2)):
        arrived(sbuf.at[at_y(d), pl.ds(2 * (1 - i), 2)], s_sib_recv.at[n])
    for d in range(1, 16):
        arrived(fb.at[lax.rem(c + 16 - d, 16)], fc_recv.at[d])
    fout_ref[...] = fb[...]
    coupling_part(0)
    zeta_done(1)
    y_combined(3)
    coupling_part(1)
    coupling_done(0)
    zeta_done(2)
    coupling_part(2)
    coupling_done(1)
    zeta_done(3)
    coupling_done(2)
    coupling_part(3)
    coupling_done(3)

    sums = jnp.sum(cross[...].reshape(768, 128).T, axis=0, keepdims=True)
    ca[c] = jnp.zeros((8, 128), F32)
    for n in range(6):
        ca[c, n:n + 1] = sums[:, n * 128:(n + 1) * 128]
    for d in range(1, 16):
        send(ca.at[c], ca.at[c], cc_send.at[d], cc_recv.at[d], r, lax.rem(c + d, 16))
    for d in range(1, 16):
        arrived(ca.at[lax.rem(c + 16 - d, 16)], cc_recv.at[d])
    cb[r] = jnp.sum(ca[...], axis=0)
    for d in range(1, 8):
        send(cb.at[r], cb.at[r], cr_send.at[d], cr_recv.at[d], lax.rem(r + d, 8), c)
    for d in range(1, 8):
        arrived(cb.at[lax.rem(r + 8 - d, 8)], cr_recv.at[d])
    cout_ref[...] = cb[...]

    @pl.when(same)
    def _():
        for copy in factor_copies(0) + [sigma_other()] + spread_copies():
            copy.wait_send()

    @pl.when(other)
    def _():
        for copy in factor_copies(1) + [sigma_copy(0), sigma_copy(1)]:
            copy.wait_send()

    for copy in pending:
        copy.wait_send()


def selected_inverse(gt, masked, sigma, fac):
    dma = pltpu.SemaphoreType.DMA
    any_space = pl.BlockSpec(memory_space=pl.ANY)
    vmem = pl.BlockSpec(memory_space=pltpu.VMEM)
    return pl.pallas_call(
        kernel,
        out_shape=(
            jax.ShapeDtypeStruct((2, 4, 2, 48, 512), F32),
            jax.ShapeDtypeStruct((16, 8, 128), F32),
            jax.ShapeDtypeStruct((8, 8, 128), F32),
        ),
        in_specs=[any_space, any_space, any_space, vmem],
        out_specs=(vmem, vmem, vmem),
        scratch_shapes=[
            pltpu.VMEM((2, 4, 2, 2, 48, 768), BF16),
            pltpu.VMEM((2, 4, 2, 384, 512), BF16),
            pltpu.VMEM((4, 4, 512, 512), BF16),
            pltpu.VMEM((NQ, 4, 4, 48, 512), F32),
            pltpu.VMEM((NQ, 2, 2, 48, 512), F32),
            pltpu.VMEM((NQ, 2, 4, 48, 512), F32),
            pltpu.VMEM((NQ, 4, 4, 48, 512), BF16),
            pltpu.VMEM((NQ, 3, 192, 512), BF16),
            pltpu.VMEM((NQ, 3, 192, 512), BF16),
            pltpu.VMEM((2, 4, 2, 48, 128), F32),
            pltpu.VMEM((8, 8, 128), F32),
            pltpu.VMEM((16, 8, 128), F32),
            pltpu.VMEM((16, 8, 128), F32),
            pltpu.VMEM((8, 8, 128), F32),
            dma((3,)),
            dma((4,)), dma((4, 2)), dma((4,)), dma((2,)),
            dma((6,)), dma((6,)), dma((4,)), dma((4,)),
            dma((2,)), dma((2,)), dma((6,)), dma((6,)), dma((4,)), dma((4,)),
            dma((NQ, 6)), dma((NQ, 6)), dma((NQ, 3)), dma((NQ, 3)), dma((NQ, 3)), dma((NQ, 3)),
            dma((8,)), dma((8,)), dma((16,)), dma((16,)),
            dma((8,)), dma((8,)), dma((16,)), dma((16,)),
        ],
        compiler_params=pltpu.CompilerParams(
            collective_id=0, has_side_effects=True, vmem_limit_bytes=60 * 1024 * 1024
        ),
    )(gt, masked, sigma, fac)


def per_device(sigma_ss, l_cs, g_cc, pattern, sup_sizes, owner):
    local_rows = l_cs.shape[0]
    row_start = lax.axis_index("row") * local_rows
    row_ends = jnp.cumsum(sup_sizes) * BLK
    child_rows = row_start + jnp.arange(local_rows, dtype=jnp.int32)
    supernode = jnp.sum((child_rows[:, None] >= row_ends[None, :]).astype(jnp.int32), axis=1)
    one_hot = (supernode[:, None] == jnp.arange(NSUP, dtype=jnp.int32)[None, :]).astype(F32)
    block_mask = jnp.dot(one_hot, pattern.astype(F32), precision=lax.Precision.HIGHEST)
    full_mask = jnp.repeat(block_mask, BLK, axis=1)
    masked = (l_cs.astype(F32) * full_mask).astype(BF16)
    g_wide = g_cc.astype(F32)
    fac = jnp.sum(g_wide * g_wide, axis=0).reshape(3, 128)
    fac = jnp.concatenate([fac, jnp.zeros((5, 128), F32)], axis=0)
    gt = g_cc.T.reshape(4, 2, 48, 768)
    sigma = sigma_ss.reshape(512, 2, 512).transpose(1, 0, 2)
    coupling, factor_sums, cross_sums = selected_inverse(gt, masked.reshape(2, 384, 512), sigma, fac)
    sel_cs = full_mask * coupling.reshape(768, 512)
    variance = factor_sums[:, :3].reshape(6144) - cross_sums[:, :6].reshape(6144)
    log_all = jnp.log(variance)
    positions = jnp.arange(6144, dtype=jnp.int32)
    log_var = jnp.sum(
        jnp.where(owner[:, None] == positions[None, :], log_all[None, :], 0.0), axis=1
    )
    return (sel_cs, log_var)


def solution(mesh):
    in_specs = (
        P("col", "row"),
        P("row", "col"),
        P("row", "col"),
        P(None, "col"),
        P(),
        P(("row", "col")),
    )
    out_specs = (P("row", "col"), P(("row", "col")))
    return jax.shard_map(
        per_device, mesh=mesh, in_specs=in_specs, out_specs=out_specs, check_vma=False
    )
```

time: 412 us -> 167 us (0.41)
  waiting for transfers between devices: 300 us -> 0 us
  Pallas kernels: 0 us -> 153 us
  blocking collectives: 64.8 us -> 0 us
  matrix products: 24.9 us -> 1.07 us
  between operations: 13.9 us -> 0.76 us
    all_gather x3 -> x0, waiting for transfers between devices: 227 us -> none  [the longest x1 92.6 us: per_device(): lax.all_gather(zeta, 'col', axis=1, tiled=True)]
    pallas_call x0 -> x1, Pallas kernels: none -> 153 us  [selected_inverse(): pl.pallas_call(kernel, out_shape=(jax.ShapeDtypeStruct((2, 4, 2, 48, 512)...]
    reduce_scatter x1 -> x0, waiting for transfers between devices: 71.3 us -> none  [per_device(): lax.psum_scatter(lax.dot_general(columns, masked, (((0,), (0,)), ((), ())...]
    psum x1 -> x0, blocking collectives: 64.8 us -> none  [per_device(): variance = lax.psum(factor_vector + cross_vector, ('row', 'col'))]
    dot_general x3 -> x1, matrix products: 24.9 us -> 1.07 us  [per_device(): jnp.dot(one_hot, pattern.astype(F32), precision=lax.Precision.HIGHEST)]
  transfers between devices with their start and end apart: 4 -> 0, of which waited for: 4 -> 0; matrix products, arithmetic and copies ran while one was open for 1% -> 0% of each run, Pallas kernels for 0% -> 0%
where the time goes in v1:
time: 167 us
  Pallas kernels  153 us (92%)
  other arithmetic  6.54 us (4%)
  local copies, waits for them, and re-layouts  6.31 us (4%)
    pallas_call x1, Pallas kernels, selected_inverse(): pl.pallas_call(kernel, out_shape=(jax.ShapeDtypeStruct((2, 4, 2, 48, 512)...  153 us

profile of v1, /device:TPU:1, one launch (start us, length us, event | category | flops | bytes accessed | tf_op | source)
XLA Modules:
  0.0 167.2 jit_solution(1586297980746705773)
XLA Ops:
  0.6 0.0 copy-start
  0.6 1.3 multiply_reduce_fusion
  2.0 0.6 concatenate.3.fac_ref
  2.6 0.7 copy.16
  3.3 0.1 multiply_reduce_fusion.1
  3.5 0.1 convert_reduce_fusion
  3.5 1.1 fusion.1
  4.6 2.1 %copy.18 = bf16[384,768]{1,0:T(8,128)(2,1)} copy(bf16[384,768]{0,1:T(8,128)(2,1)} %bitcast.21) | data formatting | bytes 1179648 | tf_op jit(solution)/shard_map/transpose | solution.py:411
  6.8 0.0 copy-done
  6.8 0.5 copy.19
  7.3 0.0 copy-start.1
  7.3 1.3 copy.20
  8.6 0.9 broadcast_in_dim.10
  9.6 0.0 copy-done.1
  9.6 1.2 fusion
  10.8 152.5 %shard_map.77 = (f32[2,4,2,48,512]{4,3,2,1,0:T(8,128)}, f32[16,8,128]{2,1,0:T(8,128)}, f32[8,8,128]{2,1,0:T(8,128)}) custom-call(bf16[4,2,48,768]{3,2,1,0:T(8,128)(2,1)} %bitcast.22, bf16[2,384,512]{2,1,0:T(8,128)(2,1)} %bitcast.20, bf16[2,512,512]{2,1,0:T(8,128)(2,1)} %bitcast.18, f32[8,128]{1,0:T(8,128)} %concatenate.3.fac_ref), custom_call_target="tpu_custom_call" | custom-call | tf_op jit(solution)/shard_map/pallas_call | solution.py:360
  163.3 0.0 copy-start.2
  163.3 0.0 copy-start.3
  163.3 0.0 copy-start.4
  163.4 2.9 %bitcast_multiply_fusion = f32[768,512]{1,0:T(8,128)} fusion(f32[2,4,2,48,512]{4,3,2,1,0:T(8,128)} %get-tuple-element.5, f32[96,8,4,128]{3,2,1,0:T(4,128)S(1)} %bitcast.17), kind=kLoop, calls=%fused_computation | loop fusion | flops 393216 | bytes 4718592 | tf_op jit(solution)/shard_map/mul | solution.py:414
  166.3 0.0 copy-done.2
  166.3 0.0 copy-done.3
  166.3 0.0 copy-done.4
  166.4 0.8 select_reduce_fusion
  (6 shorter events, 0.1 us)
Async XLA Ops:
  0.6 6.1 %copy-start = (bf16[512,1024]{1,0:T(8,128)(2,1)S(1)}, bf16[512,1024]{1,0:T(8,128)(2,1)}, u32[]{:S(2)}) copy-start(bf16[512,1024]{1,0:T(8,128)(2,1)} %param.6) | copy-start | bytes 3145732
  7.3 2.3 %copy-start.1 = (bf16[768,512]{1,0:T(8,128)(2,1)S(1)}, bf16[768,512]{1,0:T(8,128)(2,1)}, u32[]{:S(2)}) copy-start(bf16[768,512]{1,0:T(8,128)(2,1)} %param.7) | copy-start | bytes 2359300
  163.3 3.0 %copy-start.2 = (f32[8,8,128]{2,1,0:T(8,128)S(1)}, f32[8,8,128]{2,1,0:T(8,128)}, u32[]{:S(2)}) copy-start(f32[8,8,128]{2,1,0:T(8,128)} %get-tuple-element.7) | copy-start | bytes 98308
  163.3 3.0 %copy-start.3 = (f32[16,8,128]{2,1,0:T(8,128)S(1)}, f32[16,8,128]{2,1,0:T(8,128)}, u32[]{:S(2)}) copy-start(f32[16,8,128]{2,1,0:T(8,128)} %get-tuple-element.6) | copy-start | bytes 196612
  163.3 3.0 %copy-start.4 = (s32[48]{0:T(128)S(1)}, s32[48]{0:T(128)}, u32[]{:S(2)}) copy-start(s32[48]{0:T(128)} %param.11) | copy-start | bytes 580

commit v2 on v1

v2 whole, which is shorter than its diff:
```python
import jax
import jax.numpy as jnp
from jax import lax
from jax.experimental import pallas as pl
from jax.experimental.pallas import tpu as pltpu
from jax.sharding import PartitionSpec as P

NSUP = 16
MESH = pl.DeviceIdType.MESH
F32 = jnp.float32
BF16 = jnp.bfloat16
NQ = 4
FAR_ORDER = (2, 1, 3)


def kernel(
    sigma_ref, l_ref, g_ref, pattern_ref, sizes_ref, owner_ref,
    out_ref, log_ref,
    gt_ref, gbuf, mbuf, sbuf, acc, ysend, yrecv, zc, pbuf, rz, cross, fac_ref, fa, ca, cb,
    local_sem, ga_send, ga_recv, gg_send, gg_recv,
    m_send, m_recv, m_sib_send, m_sib_recv,
    sa_send, sa_recv, s_send, s_recv, s_sib_send, s_sib_recv,
    y_send, y_recv, x_send, x_recv, z_send, z_recv,
    fr_send, fr_recv, cr_send, cr_recv, cc_send, cc_recv,
):
    r = lax.axis_index("row")
    c = lax.axis_index("col")
    y, i = r // 2, r % 2
    x, z = c // 4, c % 4
    sib = 2 * y + 1 - i
    t = z // 2
    same = i == t
    other = i != t

    def at_x(d):
        return lax.rem(x + d, 4)

    def at_y(d):
        return lax.rem(y + d, 4)

    def at_z(d):
        return lax.rem(z + d, 4)

    def remote(src, dst, send, recv, row, col):
        return pltpu.make_async_remote_copy(
            src_ref=src, dst_ref=dst, send_sem=send, recv_sem=recv,
            device_id=(row, col), device_id_type=MESH,
        )

    def arrived(dst, recv):
        pltpu.make_async_copy(dst, dst, recv).wait()

    pending = []

    def send(*args):
        copy = remote(*args)
        copy.start()
        pending.append(copy)

    barrier = pltpu.get_barrier_semaphore()
    partners = [(r, lax.rem(c + d, 16)) for d in range(1, 16)]
    partners += [(lax.rem(r + d, 8), c) for d in range(1, 8)]
    partners += [(sib, 4 * at_x(d) + z) for d in range(1, 4)]
    partners += [(sib, 4 * x + at_z(d)) for d in range(1, 4)]
    for partner in partners:
        pl.semaphore_signal(barrier, inc=1, device_id=partner, device_id_type=MESH)

    ends, total_size = [], jnp.int32(0)
    for s in range(NSUP):
        total_size = total_size + sizes_ref[s]
        ends.append(total_size)
    block_mask = []
    for n in range(6):
        place = jnp.int32(0)
        for s in range(NSUP):
            place = place + (ends[s] <= 6 * r + n).astype(jnp.int32)
        place = jnp.minimum(place, NSUP - 1)
        block_mask.append([pattern_ref[place, m].astype(F32) for m in range(4)])

    gt_ref[...] = g_ref[...].T.reshape(4, 2, 48, 768)
    wide = g_ref[...].astype(F32)
    squares = jnp.sum(wide * wide, axis=0, keepdims=True)
    fac_ref[...] = jnp.zeros((8, 128), F32)
    for n in range(3):
        fac_ref[n:n + 1] = squares[:, n * 128:(n + 1) * 128]

    pl.semaphore_wait(barrier, len(partners))

    fa[r] = fac_ref[...]
    for d in range(1, 8):
        send(fac_ref, fa.at[r], fr_send.at[d], fr_recv.at[d], lax.rem(r + d, 8), c)

    def factor_dst():
        return gbuf.at[lax.rem(z, 2), x, i]

    def factor_copies(rel):
        copies = []
        for d in range(0 if rel else 1, 4):
            copies.append(remote(
                gt_ref.at[at_x(d)], factor_dst(), ga_send.at[d], ga_recv.at[d, rel],
                2 * y + t, 4 * at_x(d) + z,
            ))
        return copies

    @pl.when(same)
    def _():
        pltpu.make_async_copy(gt_ref.at[x], factor_dst(), local_sem.at[0]).start()
        for copy in factor_copies(0):
            copy.start()

    @pl.when(other)
    def _():
        for copy in factor_copies(1):
            copy.start()

    def sigma_copy(l):
        return remote(
            sigma_ref.at[:, pl.ds(l * 512, 512)], sbuf.at[y, z],
            sa_send.at[l], sa_recv.at[lax.rem(z, 2)], 2 * y + t, 4 * x + 2 * i + l,
        )

    def sigma_own():
        return pltpu.make_async_copy(sigma_ref.at[:, pl.ds(pl.multiple_of(lax.rem(z, 2) * 512, 512), 512)], sbuf.at[y, z], local_sem.at[1])

    def sigma_other():
        l = 1 - lax.rem(z, 2)
        return remote(
            sigma_ref.at[:, pl.ds(pl.multiple_of(l * 512, 512), 512)], sbuf.at[y, z],
            sa_send.at[l], sa_recv.at[lax.rem(z, 2)], 2 * y + t, 4 * x + 2 * i + l,
        )

    @pl.when(same)
    def _():
        sigma_own().start()
        sigma_other().start()

    @pl.when(other)
    def _():
        sigma_copy(0).start()
        sigma_copy(1).start()

    def ring_first(src, slot, snd, rcv, right, left, me):
        send(src(0), slot(me, 0), snd.at[0], rcv.at[0], *right)
        send(src(1), slot(me, 1), snd.at[2], rcv.at[2], *left)
        send(src(1), slot(me, 1), snd.at[1], rcv.at[1], *right)
        send(src(0), slot(me, 0), snd.at[3], rcv.at[3], *left)

    def ring_forward(slot, snd, rcv, right, left, at):
        arrived(slot(at(3), 0), rcv.at[0])
        send(slot(at(3), 0), slot(at(3), 0), snd.at[4], rcv.at[4], *right)
        arrived(slot(at(1), 1), rcv.at[2])
        send(slot(at(1), 1), slot(at(1), 1), snd.at[5], rcv.at[5], *left)

    def ring_rest(slot, rcv, at):
        arrived(slot(at(3), 1), rcv.at[1])
        arrived(slot(at(1), 0), rcv.at[3])

    def ring_far(slot, rcv, at):
        arrived(slot(at(2), 0), rcv.at[4])
        arrived(slot(at(2), 1), rcv.at[5])

    x_right, x_left = (r, 4 * at_x(1) + z), (r, 4 * at_x(3) + z)
    y_right, y_left = (2 * at_y(1) + i, c), (2 * at_y(3) + i, c)

    def m_slot(place, half):
        return mbuf.at[i, place, half]

    def m_share(n, place):
        send(mbuf.at[i, place], mbuf.at[i, place], m_sib_send.at[n], m_sib_recv.at[n], sib, c)

    def s_slot(place, half):
        return sbuf.at[place, 2 * i + half]

    def s_share(n, place):
        block = sbuf.at[place, pl.ds(2 * i, 2)]
        send(block, block, s_sib_send.at[n], s_sib_recv.at[n], sib, c)

    for n in range(6):
        for m in range(4):
            block = l_ref[n * 128:(n + 1) * 128, m * 128:(m + 1) * 128].astype(F32)
            mbuf[i, x, n // 3, (n % 3) * 128:(n % 3 + 1) * 128, m * 128:(m + 1) * 128] = (
                block * block_mask[n][m]
            ).astype(BF16)
    ring_first(lambda h: m_slot(x, h), m_slot, m_send, m_recv, x_right, x_left, x)
    m_share(0, x)
    @pl.when(same)
    def _():
        sigma_own().wait()
        m = 1 - lax.rem(z, 2)
        arrived(sbuf.at[y, 2 * i + m], sa_recv.at[m])

    @pl.when(other)
    def _():
        arrived(sbuf.at[y, 2 * i], sa_recv.at[0])
        arrived(sbuf.at[y, 2 * i + 1], sa_recv.at[1])

    ring_first(lambda h: s_slot(y, h), s_slot, s_send, s_recv, y_right, y_left, y)
    s_share(0, y)

    def spread_copies():
        slot = gbuf.at[lax.rem(z, 2)]
        return [
            remote(slot, slot, gg_send.at[d], gg_recv.at[lax.rem(z, 2)], r, 4 * x + at_z(d))
            for d in FAR_ORDER
        ]

    @pl.when(same)
    def _():
        pltpu.make_async_copy(gt_ref.at[x], factor_dst(), local_sem.at[0]).wait()
        for d in range(4):
            for rel in range(2):
                if d or rel:
                    src_core = 1 - i if rel else i
                    arrived(gbuf.at[lax.rem(z, 2), at_x(4 - d), src_core], ga_recv.at[d, rel])
        for copy in spread_copies():
            copy.start()

    ring_forward(m_slot, m_send, m_recv, x_right, x_left, at_x)
    ring_rest(m_slot, m_recv, at_x)
    m_share(1, at_x(3))
    m_share(2, at_x(1))
    ring_forward(s_slot, s_send, s_recv, y_right, y_left, at_y)
    ring_rest(s_slot, s_recv, at_y)
    s_share(1, at_y(3))
    s_share(2, at_y(1))

    ring_far(m_slot, m_recv, at_x)
    m_share(3, at_x(2))
    for zl in range(2):
        @pl.when(z != 2 * i + zl)
        def _():
            arrived(gbuf.at[zl], gg_recv.at[zl])
    for n, d in enumerate((0, 3, 1, 2)):
        arrived(mbuf.at[1 - i, at_x(d)], m_sib_recv.at[n])

    def zeta_part(q):
        zl, half = q // 2, q % 2
        g0 = gbuf[zl, :, 0, half].reshape(192, 768)
        g1 = gbuf[zl, :, 1, half].reshape(192, 768)

        def step(k, carry):
            total = jnp.dot(g0, mbuf[0, k].reshape(768, 512), preferred_element_type=F32)
            total += jnp.dot(g1, mbuf[1, k].reshape(768, 512), preferred_element_type=F32)
            acc[q, :, k] = total.reshape(4, 48, 512)
            return carry

        lax.fori_loop(0, 4, step, 0)

    def zeta_send(q):
        for d in FAR_ORDER:
            parts = [acc[q, at_y(d), k] for k in range(4)]
            top = jnp.abs(parts[0])
            for part in parts[1:]:
                top = jnp.maximum(top, jnp.abs(part))
            top = jnp.max(top, axis=1, keepdims=True)
            power = jnp.floor(jnp.log2(jnp.maximum(top, 1e-30)) + 1.01)
            up = jnp.exp2(15.0 - power)
            for k in range(4):
                code = jnp.round(parts[k] * up).astype(jnp.int32).astype(jnp.int16)
                ysend[q, d - 1, :, k * 512:(k + 1) * 512] = code
            ysend[q, d - 1, :, 2048:] = jnp.broadcast_to(
                power.astype(jnp.int32), (48, 128)
            ).astype(jnp.int16)
            send(
                ysend.at[q, d - 1], yrecv.at[q, d - 1],
                y_send.at[q, d - 1], y_recv.at[q, d - 1], 2 * at_y(d) + i, c,
            )

    def zeta_done(q):
        for d in range(3):
            arrived(yrecv.at[q, d], y_recv.at[q, d])
        down = []
        for d in range(3):
            power = yrecv[q, d, :, 2048:].astype(jnp.int32).astype(F32)
            down.append(jnp.exp2(power - 15.0)[:, 0:1])
        for k in range(4):
            total = acc[q, y, k]
            for d in range(3):
                code = yrecv[q, d, :, k * 512:(k + 1) * 512]
                total += code.astype(jnp.int32).astype(F32) * down[d]
            zc[q, k, x] = total.astype(BF16)
        for d in FAR_ORDER:
            send(zc.at[q, :, x], zc.at[q, :, x], x_send.at[q, d - 1], x_recv.at[q, d - 1], r, 4 * at_x(d) + z)

    def product(q, zt):
        total = None
        for k in range(4):
            part = lax.dot_general(
                zc[q, k].reshape(192, 512), sbuf[k, zt],
                (((1,), (1,)), ((), ())), preferred_element_type=F32,
            )
            total = part if total is None else total + part
        return total

    def first_row(q, place):
        return (q // 2) * 384 + place * 96 + (q % 2) * 48

    def put_rows(q, total):
        for place in range(4):
            out_ref[pl.ds(first_row(q, place), 48), :] = total[place * 48:(place + 1) * 48]

    def coupling_part(q):
        for d in range(1, 4):
            arrived(zc.at[q, :, at_x(4 - d)], x_recv.at[q, d - 1])
        for d in FAR_ORDER:
            pbuf[q, d - 1] = product(q, at_z(d)).astype(BF16)
            send(pbuf.at[q, d - 1], rz.at[q, d - 1], z_send.at[q, d - 1], z_recv.at[q, d - 1], r, 4 * x + at_z(d))
        put_rows(q, product(q, z))

    def coupling_done(q):
        for d in range(3):
            arrived(rz.at[q, d], z_recv.at[q, d])
        total = jnp.concatenate(
            [out_ref[pl.ds(first_row(q, place), 48), :] for place in range(4)], axis=0
        )
        total += rz[q, 0].astype(F32) + rz[q, 1].astype(F32) + rz[q, 2].astype(F32)
        total = -total
        put_rows(q, total)
        terms = total * zc[q, x].reshape(192, 512).astype(F32)
        terms = terms[:, 0:128] + terms[:, 128:256] + terms[:, 256:384] + terms[:, 384:512]
        for place in range(4):
            cross[pl.ds(first_row(q, place), 48), :] = terms[place * 48:(place + 1) * 48]

    zeta_part(0)
    zeta_send(0)
    ring_far(s_slot, s_recv, at_y)
    s_share(3, at_y(2))
    zeta_part(1)
    zeta_send(1)
    zeta_done(0)
    zeta_part(2)
    zeta_send(2)
    zeta_done(1)
    zeta_part(3)
    zeta_send(3)
    for n, d in enumerate((0, 3, 1, 2)):
        arrived(sbuf.at[at_y(d), pl.ds(2 * (1 - i), 2)], s_sib_recv.at[n])
    coupling_part(0)
    zeta_done(2)
    coupling_part(1)
    coupling_done(0)
    zeta_done(3)
    coupling_part(2)
    coupling_done(1)
    for d in range(1, 8):
        arrived(fa.at[lax.rem(r + 8 - d, 8)], fr_recv.at[d])
    ca[c, 8:16] = jnp.sum(fa[...], axis=0)
    ca[c, 0:8] = jnp.zeros((8, 128), F32)
    coupling_part(3)
    coupling_done(2)
    coupling_done(3)

    sums = jnp.sum(cross[...].T, axis=0, keepdims=True)
    for n in range(6):
        ca[c, n:n + 1] = sums[:, n * 128:(n + 1) * 128]
    for d in range(1, 16):
        send(ca.at[c], ca.at[c], cc_send.at[d], cc_recv.at[d], r, lax.rem(c + d, 16))
    for n in range(6):
        for m in range(4):
            rows, columns = slice(n * 128, (n + 1) * 128), slice(m * 128, (m + 1) * 128)
            out_ref[rows, columns] = out_ref[rows, columns] * block_mask[n][m]
    for d in range(1, 16):
        arrived(ca.at[lax.rem(c + 16 - d, 16)], cc_recv.at[d])
    cb[r] = jnp.sum(ca[:, 0:8], axis=0)
    for d in range(1, 8):
        send(cb.at[r], cb.at[r], cr_send.at[d], cr_recv.at[d], lax.rem(r + d, 8), c)
    wanted = jnp.broadcast_to(owner_ref[...].astype(F32), (128, 48)).T
    lanes = lax.broadcasted_iota(jnp.int32, (48, 128), 1).astype(F32)
    for d in range(1, 8):
        arrived(cb.at[lax.rem(r + 8 - d, 8)], cr_recv.at[d])
    picked = jnp.zeros((48, 128), F32)
    for n in range(48):
        row = jnp.log(ca[n // 3, 8 + n % 3:9 + n % 3] - cb[n // 6, n % 6:n % 6 + 1])
        picked = jnp.where(wanted - float(128 * n) == lanes, row, picked)
    log_ref[...] = jnp.sum(picked.T, axis=0, keepdims=True)

    @pl.when(same)
    def _():
        for copy in factor_copies(0) + [sigma_other()] + spread_copies():
            copy.wait_send()

    @pl.when(other)
    def _():
        for copy in factor_copies(1) + [sigma_copy(0), sigma_copy(1)]:
            copy.wait_send()

    for copy in pending:
        copy.wait_send()


def per_device(sigma_ss, l_cs, g_cc, pattern, sup_sizes, owner):
    dma = pltpu.SemaphoreType.DMA
    any_space = pl.BlockSpec(memory_space=pl.ANY)
    vmem = pl.BlockSpec(memory_space=pltpu.VMEM)
    smem = pl.BlockSpec(memory_space=pltpu.SMEM)
    sel_cs, log_var = pl.pallas_call(
        kernel,
        out_shape=(
            jax.ShapeDtypeStruct((768, 512), F32),
            jax.ShapeDtypeStruct((1, 48), F32),
        ),
        in_specs=[any_space, vmem, vmem, smem, smem, vmem],
        out_specs=(vmem, vmem),
        scratch_shapes=[
            pltpu.VMEM((4, 2, 48, 768), BF16),
            pltpu.VMEM((2, 4, 2, 2, 48, 768), BF16),
            pltpu.VMEM((2, 4, 2, 384, 512), BF16),
            pltpu.VMEM((4, 4, 512, 512), BF16),
            pltpu.VMEM((NQ, 4, 4, 48, 512), F32),
            pltpu.VMEM((NQ, 3, 48, 2176), jnp.int16),
            pltpu.VMEM((NQ, 3, 48, 2176), jnp.int16),
            pltpu.VMEM((NQ, 4, 4, 48, 512), BF16),
            pltpu.VMEM((NQ, 3, 192, 512), BF16),
            pltpu.VMEM((NQ, 3, 192, 512), BF16),
            pltpu.VMEM((768, 128), F32),
            pltpu.VMEM((8, 128), F32),
            pltpu.VMEM((8, 8, 128), F32),
            pltpu.VMEM((16, 16, 128), F32),
            pltpu.VMEM((8, 8, 128), F32),
            dma((3,)),
            dma((4,)), dma((4, 2)), dma((4,)), dma((2,)),
            dma((6,)), dma((6,)), dma((4,)), dma((4,)),
            dma((2,)), dma((2,)), dma((6,)), dma((6,)), dma((4,)), dma((4,)),
            dma((NQ, 3)), dma((NQ, 3)), dma((NQ, 3)), dma((NQ, 3)), dma((NQ, 3)), dma((NQ, 3)),
            dma((8,)), dma((8,)),
            dma((8,)), dma((8,)), dma((16,)), dma((16,)),
        ],
        compiler_params=pltpu.CompilerParams(
            collective_id=0, has_side_effects=True, vmem_limit_bytes=60 * 1024 * 1024
        ),
    )(sigma_ss, l_cs, g_cc, pattern, sup_sizes, owner.reshape(1, 48))
    return (sel_cs, log_var.reshape(48))


def solution(mesh):
    in_specs = (
        P("col", "row"),
        P("row", "col"),
        P("row", "col"),
        P(None, "col"),
        P(),
        P(("row", "col")),
    )
    out_specs = (P("row", "col"), P(("row", "col")))
    return jax.shard_map(
        per_device, mesh=mesh, in_specs=in_specs, out_specs=out_specs, check_vma=False
    )
```

time: 167 us -> 136 us (0.81)
  Pallas kernels: 153 us -> 131 us
  other arithmetic: 6.54 us -> 0 us
  local copies, waits for them, and re-layouts: 6.31 us -> 4.54 us
    pallas_call x1, Pallas kernels: 153 us -> 131 us  [per_device(): pl.pallas_call(kernel, out_shape=(jax.ShapeDtypeStruct((768, 512), F32),...]
    unnamed x11 -> x5, local copies, waits for them, and re-layouts: 0.56 us -> 4.54 us
    mul x2 -> x0, other arithmetic: 3.04 us -> none  [the longest x1 2.92 us: per_device(): sel_cs = full_mask * coupling.reshape(768, 512)]
    reduce_sum x3 -> x0, other arithmetic: 2.26 us -> none  [the longest x1 1.33 us: per_device(): fac = jnp.sum(g_wide * g_wide, axis=0).reshape(3, 128)]
    transpose x1 -> x0, local copies, waits for them, and re-layouts: 2.13 us -> none  [per_device(): gt = g_cc.T.reshape(4, 2, 48, 768)]
where the time goes in v2:
time: 136 us
  Pallas kernels  131 us (96%)
  local copies, waits for them, and re-layouts  4.54 us (3%)
    pallas_call x1, Pallas kernels, per_device(): pl.pallas_call(kernel, out_shape=(jax.ShapeDtypeStruct((768, 512), F32),...  131 us
    unnamed x5, local copies, waits for them, and re-layouts  4.54 us

profile of v2, /device:TPU:1, one launch (start us, length us, event | category | flops | bytes accessed | tf_op | source)
XLA Modules:
  0.0 136.0 jit_solution(9236738527977378634)
XLA Ops:
  0.6 1.4 copy.8.pattern_ref
  2.0 130.8 %shard_map.77 = (f32[768,512]{1,0:T(8,128)}, f32[1,48]{1,0:T(1,128)}) custom-call(bf16[512,1024]{1,0:T(8,128)(2,1)} %sigma_ref.1, bf16[768,512]{1,0:T(8,128)(2,1)} %l_ref.1, bf16[768,384]{1,0:T(8,128)(2,1)} %g_ref.1, s32[16,4]{1,0:T(8,128)} %copy.8.pattern_ref, s32[16]{0:T(128)} %sizes_ref.1, s32[1,48]{1,0:T(1,128)} %bitcast.2), custom_call_target="tpu_custom_call" | custom-call | tf_op jit(solution)/shard_map/pallas_call | solution.py:396
  132.8 0.0 copy-start
  132.8 2.7 %copy.11 = f32[768,512]{1,0:T(8,128)} copy(f32[768,512]{1,0:T(8,128)} %get-tuple-element.8) | data formatting | bytes 3145728
  135.5 0.0 copy-done
  135.5 0.5 copy.12
Async XLA Ops:
  132.8 2.7 %copy-start = (f32[1,48]{1,0:T(1,128)S(1)}, f32[1,48]{1,0:T(1,128)}, u32[]{:S(2)}) copy-start(f32[1,48]{1,0:T(1,128)} %get-tuple-element.5) | copy-start | bytes 580

commit v3 on v2

--- a/solution.py
+++ b/solution.py
@@ -9,7 +9,8 @@
 MESH = pl.DeviceIdType.MESH
 F32 = jnp.float32
 BF16 = jnp.bfloat16
-NQ = 4
+CHUNKS = ((0, 0, 48), (0, 48, 48), (1, 0, 48), (1, 48, 32), (1, 80, 16))
+NQ = len(CHUNKS)
 FAR_ORDER = (2, 1, 3)
 
 
@@ -75,9 +76,16 @@
         for s in range(NSUP):
             place = place + (ends[s] <= 6 * r + n).astype(jnp.int32)
         place = jnp.minimum(place, NSUP - 1)
-        block_mask.append([pattern_ref[place, m].astype(F32) for m in range(4)])
-
-    gt_ref[...] = g_ref[...].T.reshape(4, 2, 48, 768)
+        row = pattern_ref[pl.ds(place, 1), :].astype(F32)
+        block_mask.append([row[:, m:m + 1] for m in range(4)])
+
+    for n in range(6):
+        for m in range(4):
+            block = l_ref[n * 128:(n + 1) * 128, m * 128:(m + 1) * 128].astype(F32)
+            mbuf[i, x, n // 3, (n % 3) * 128:(n % 3 + 1) * 128, m * 128:(m + 1) * 128] = (
+                block * block_mask[n][m]
+            ).astype(BF16)
+    gt_ref[...] = g_ref[...].T.reshape(4, 96, 768)
     wide = g_ref[...].astype(F32)
     squares = jnp.sum(wide * wide, axis=0, keepdims=True)
     fac_ref[...] = jnp.zeros((8, 128), F32)
@@ -113,31 +121,34 @@
         for copy in factor_copies(1):
             copy.start()
 
+    def sigma_part(l, half):
+        return sigma_ref.at[pl.ds(half * 256, 256), pl.ds(pl.multiple_of(l * 512, 512), 512)]
+
+    def sigma_own():
+        return [
+            pltpu.make_async_copy(sigma_part(lax.rem(z, 2), h), sbuf.at[y, z, h], local_sem.at[1 + h])
+            for h in range(2)
+        ]
+
     def sigma_copy(l):
-        return remote(
-            sigma_ref.at[:, pl.ds(l * 512, 512)], sbuf.at[y, z],
-            sa_send.at[l], sa_recv.at[lax.rem(z, 2)], 2 * y + t, 4 * x + 2 * i + l,
-        )
-
-    def sigma_own():
-        return pltpu.make_async_copy(sigma_ref.at[:, pl.ds(pl.multiple_of(lax.rem(z, 2) * 512, 512), 512)], sbuf.at[y, z], local_sem.at[1])
-
-    def sigma_other():
-        l = 1 - lax.rem(z, 2)
-        return remote(
-            sigma_ref.at[:, pl.ds(pl.multiple_of(l * 512, 512), 512)], sbuf.at[y, z],
-            sa_send.at[l], sa_recv.at[lax.rem(z, 2)], 2 * y + t, 4 * x + 2 * i + l,
-        )
+        return [
+            remote(
+                sigma_part(l, h), sbuf.at[y, z, h],
+                sa_send.at[l, h], sa_recv.at[lax.rem(z, 2), h], 2 * y + t, 4 * x + 2 * i + l,
+            )
+            for h in range(2)
+        ]
 
     @pl.when(same)
     def _():
-        sigma_own().start()
-        sigma_other().start()
+        for copy in sigma_own() + sigma_copy(1 - lax.rem(z, 2)):
+            copy.start()
 
     @pl.when(other)
     def _():
-        sigma_copy(0).start()
-        sigma_copy(1).start()
+        for first, second in zip(sigma_copy(0), sigma_copy(1)):
+            first.start()
+            second.start()
 
     def ring_first(src, slot, snd, rcv, right, left, me):
         send(src(0), slot(me, 0), snd.at[0], rcv.at[0], *right)
@@ -168,34 +179,61 @@
     def m_share(n, place):
         send(mbuf.at[i, place], mbuf.at[i, place], m_sib_send.at[n], m_sib_recv.at[n], sib, c)
 
-    def s_slot(place, half):
-        return sbuf.at[place, 2 * i + half]
-
-    def s_share(n, place):
-        block = sbuf.at[place, pl.ds(2 * i, 2)]
-        send(block, block, s_sib_send.at[n], s_sib_recv.at[n], sib, c)
-
-    for n in range(6):
-        for m in range(4):
-            block = l_ref[n * 128:(n + 1) * 128, m * 128:(m + 1) * 128].astype(F32)
-            mbuf[i, x, n // 3, (n % 3) * 128:(n % 3 + 1) * 128, m * 128:(m + 1) * 128] = (
-                block * block_mask[n][m]
-            ).astype(BF16)
+    s_block = [jnp.where(same, lax.rem(z, 2), 0)]
+    s_block.append(1 - s_block[0])
+
+    def s_slot(order):
+        return lambda place, half: sbuf.at[place, 2 * i + s_block[order], half]
+
+    def s_share(order, n, place):
+        block = sbuf.at[place, 2 * i + s_block[order]]
+        send(block, block, s_sib_send.at[order, n], s_sib_recv.at[order, n], sib, c)
+
+    def s_first(order):
+        slot = s_slot(order)
+        snd, rcv = s_send.at[order], s_recv.at[order]
+        ring_first(lambda h: slot(y, h), slot, snd, rcv, y_right, y_left, y)
+        s_share(order, 0, y)
+
+    def s_forward(order):
+        ring_forward(s_slot(order), s_send.at[order], s_recv.at[order], y_right, y_left, at_y)
+
+    def s_rest(order):
+        ring_rest(s_slot(order), s_recv.at[order], at_y)
+        s_share(order, 1, at_y(3))
+        s_share(order, 2, at_y(1))
+
+    def s_far(order):
+        ring_far(s_slot(order), s_recv.at[order], at_y)
+        s_share(order, 3, at_y(2))
+
+    def s_all():
+        for order in range(2):
+            for n, d in enumerate((0, 3, 1, 2)):
+                place = 2 * (1 - i) + sib_block[order]
+                arrived(sbuf.at[at_y(d), place], s_sib_recv.at[order, n])
+
+    sib_block = [jnp.where(other, lax.rem(z, 2), 0)]
+    sib_block.append(1 - sib_block[0])
+
     ring_first(lambda h: m_slot(x, h), m_slot, m_send, m_recv, x_right, x_left, x)
     m_share(0, x)
+
     @pl.when(same)
     def _():
-        sigma_own().wait()
-        m = 1 - lax.rem(z, 2)
-        arrived(sbuf.at[y, 2 * i + m], sa_recv.at[m])
+        for copy in sigma_own():
+            copy.wait()
 
     @pl.when(other)
     def _():
-        arrived(sbuf.at[y, 2 * i], sa_recv.at[0])
-        arrived(sbuf.at[y, 2 * i + 1], sa_recv.at[1])
-
-    ring_first(lambda h: s_slot(y, h), s_slot, s_send, s_recv, y_right, y_left, y)
-    s_share(0, y)
+        for h in range(2):
+            arrived(sbuf.at[y, 2 * i, h], sa_recv.at[0, h])
+
+    s_first(0)
+
+    for h in range(2):
+        arrived(sbuf.at[y, 2 * i + s_block[1], h], sa_recv.at[s_block[1], h])
+    s_first(1)
 
     def spread_copies():
         slot = gbuf.at[lax.rem(z, 2)]
@@ -215,14 +253,14 @@
         for copy in spread_copies():
             copy.start()
 
+    s_forward(0)
     ring_forward(m_slot, m_send, m_recv, x_right, x_left, at_x)
     ring_rest(m_slot, m_recv, at_x)
     m_share(1, at_x(3))
     m_share(2, at_x(1))
-    ring_forward(s_slot, s_send, s_recv, y_right, y_left, at_y)
-    ring_rest(s_slot, s_recv, at_y)
-    s_share(1, at_y(3))
-    s_share(2, at_y(1))
+    s_rest(0)
+    s_forward(1)
+    s_rest(1)
 
     ring_far(m_slot, m_recv, at_x)
     m_share(3, at_x(2))
@@ -234,21 +272,24 @@
         arrived(mbuf.at[1 - i, at_x(d)], m_sib_recv.at[n])
 
     def zeta_part(q):
-        zl, half = q // 2, q % 2
-        g0 = gbuf[zl, :, 0, half].reshape(192, 768)
-        g1 = gbuf[zl, :, 1, half].reshape(192, 768)
+        zl, start, rows = CHUNKS[q]
+        here = slice(start, start + rows)
+        g0 = gbuf[zl, :, 0, here].reshape(4 * rows, 768)
+        g1 = gbuf[zl, :, 1, here].reshape(4 * rows, 768)
 
         def step(k, carry):
             total = jnp.dot(g0, mbuf[0, k].reshape(768, 512), preferred_element_type=F32)
             total += jnp.dot(g1, mbuf[1, k].reshape(768, 512), preferred_element_type=F32)
-            acc[q, :, k] = total.reshape(4, 48, 512)
+            acc[zl, :, k, here] = total.reshape(4, rows, 512)
             return carry
 
         lax.fori_loop(0, 4, step, 0)
 
     def zeta_send(q):
+        zl, start, rows = CHUNKS[q]
+        here = slice(start, start + rows)
         for d in FAR_ORDER:
-            parts = [acc[q, at_y(d), k] for k in range(4)]
+            parts = [acc[zl, at_y(d), k, here] for k in range(4)]
             top = jnp.abs(parts[0])
             for part in parts[1:]:
                 top = jnp.maximum(top, jnp.abs(part))
@@ -257,98 +298,97 @@
             up = jnp.exp2(15.0 - power)
             for k in range(4):
                 code = jnp.round(parts[k] * up).astype(jnp.int32).astype(jnp.int16)
-                ysend[q, d - 1, :, k * 512:(k + 1) * 512] = code
-            ysend[q, d - 1, :, 2048:] = jnp.broadcast_to(
-                power.astype(jnp.int32), (48, 128)
+                ysend[zl, d - 1, here, k * 512:(k + 1) * 512] = code
+            ysend[zl, d - 1, here, 2048:] = jnp.broadcast_to(
+                power.astype(jnp.int32), (rows, 128)
             ).astype(jnp.int16)
             send(
-                ysend.at[q, d - 1], yrecv.at[q, d - 1],
+                ysend.at[zl, d - 1, pl.ds(start, rows)], yrecv.at[zl, d - 1, pl.ds(start, rows)],
                 y_send.at[q, d - 1], y_recv.at[q, d - 1], 2 * at_y(d) + i, c,
             )
 
     def zeta_done(q):
+        zl, start, rows = CHUNKS[q]
+        here = slice(start, start + rows)
         for d in range(3):
-            arrived(yrecv.at[q, d], y_recv.at[q, d])
+            arrived(yrecv.at[zl, d, pl.ds(start, rows)], y_recv.at[q, d])
         down = []
         for d in range(3):
-            power = yrecv[q, d, :, 2048:].astype(jnp.int32).astype(F32)
+            power = yrecv[zl, d, here, 2048:].astype(jnp.int32).astype(F32)
             down.append(jnp.exp2(power - 15.0)[:, 0:1])
         for k in range(4):
-            total = acc[q, y, k]
+            total = acc[zl, y, k, here]
             for d in range(3):
-                code = yrecv[q, d, :, k * 512:(k + 1) * 512]
+                code = yrecv[zl, d, here, k * 512:(k + 1) * 512]
                 total += code.astype(jnp.int32).astype(F32) * down[d]
-            zc[q, k, x] = total.astype(BF16)
+            zc[zl, k, x, here] = total.astype(BF16)
+        block = zc.at[zl, :, x, pl.ds(start, rows)]
         for d in FAR_ORDER:
-            send(zc.at[q, :, x], zc.at[q, :, x], x_send.at[q, d - 1], x_recv.at[q, d - 1], r, 4 * at_x(d) + z)
+            send(block, block, x_send.at[q, d - 1], x_recv.at[q, d - 1], r, 4 * at_x(d) + z)
 
     def product(q, zt):
+        zl, start, rows = CHUNKS[q]
         total = None
         for k in range(4):
             part = lax.dot_general(
-                zc[q, k].reshape(192, 512), sbuf[k, zt],
+                zc[zl, k, :, start:start + rows].reshape(4 * rows, 512), sbuf[k, zt].reshape(512, 512),
                 (((1,), (1,)), ((), ())), preferred_element_type=F32,
             )
             total = part if total is None else total + part
         return total
 
-    def first_row(q, place):
-        return (q // 2) * 384 + place * 96 + (q % 2) * 48
-
-    def put_rows(q, total):
-        for place in range(4):
-            out_ref[pl.ds(first_row(q, place), 48), :] = total[place * 48:(place + 1) * 48]
+    def row_places(q):
+        zl, start, rows = CHUNKS[q]
+        return [(pl.ds(zl * 384 + p * 96 + start, rows), slice(p * rows, (p + 1) * rows)) for p in range(4)]
 
     def coupling_part(q):
+        zl, start, rows = CHUNKS[q]
+        here = pl.ds(start, rows)
         for d in range(1, 4):
-            arrived(zc.at[q, :, at_x(4 - d)], x_recv.at[q, d - 1])
+            arrived(zc.at[zl, :, at_x(4 - d), here], x_recv.at[q, d - 1])
         for d in FAR_ORDER:
-            pbuf[q, d - 1] = product(q, at_z(d)).astype(BF16)
-            send(pbuf.at[q, d - 1], rz.at[q, d - 1], z_send.at[q, d - 1], z_recv.at[q, d - 1], r, 4 * x + at_z(d))
-        put_rows(q, product(q, z))
+            pbuf[zl, d - 1, :, start:start + rows] = product(q, at_z(d)).astype(BF16).reshape(4, rows, 512)
+            send(
+                pbuf.at[zl, d - 1, :, here], rz.at[zl, d - 1, :, here],
+                z_send.at[q, d - 1], z_recv.at[q, d - 1], r, 4 * x + at_z(d),
+            )
+        total = product(q, z)
+        for place, part in row_places(q):
+            out_ref[place, :] = total[part]
 
     def coupling_done(q):
+        zl, start, rows = CHUNKS[q]
         for d in range(3):
-            arrived(rz.at[q, d], z_recv.at[q, d])
-        total = jnp.concatenate(
-            [out_ref[pl.ds(first_row(q, place), 48), :] for place in range(4)], axis=0
-        )
-        total += rz[q, 0].astype(F32) + rz[q, 1].astype(F32) + rz[q, 2].astype(F32)
-        total = -total
-        put_rows(q, total)
-        terms = total * zc[q, x].reshape(192, 512).astype(F32)
-        terms = terms[:, 0:128] + terms[:, 128:256] + terms[:, 256:384] + terms[:, 384:512]
-        for place in range(4):
-            cross[pl.ds(first_row(q, place), 48), :] = terms[place * 48:(place + 1) * 48]
-
-    zeta_part(0)
-    zeta_send(0)
-    ring_far(s_slot, s_recv, at_y)
-    s_share(3, at_y(2))
-    zeta_part(1)
-    zeta_send(1)
-    zeta_done(0)
-    zeta_part(2)
-    zeta_send(2)
-    zeta_done(1)
-    zeta_part(3)
-    zeta_send(3)
-    for n, d in enumerate((0, 3, 1, 2)):
-        arrived(sbuf.at[at_y(d), pl.ds(2 * (1 - i), 2)], s_sib_recv.at[n])
-    coupling_part(0)
-    zeta_done(2)
-    coupling_part(1)
-    coupling_done(0)
-    zeta_done(3)
-    coupling_part(2)
-    coupling_done(1)
-    for d in range(1, 8):
-        arrived(fa.at[lax.rem(r + 8 - d, 8)], fr_recv.at[d])
-    ca[c, 8:16] = jnp.sum(fa[...], axis=0)
-    ca[c, 0:8] = jnp.zeros((8, 128), F32)
-    coupling_part(3)
-    coupling_done(2)
-    coupling_done(3)
+            arrived(rz.at[zl, d, :, pl.ds(start, rows)], z_recv.at[q, d])
+        for p, (place, part) in enumerate(row_places(q)):
+            total = out_ref[place, :]
+            for d in range(3):
+                total += rz[zl, d, p, start:start + rows].astype(F32)
+            total = -total
+            out_ref[place, :] = total
+            terms = total * zc[zl, x, p, start:start + rows].astype(F32)
+            cross[place, :] = terms[:, 0:128] + terms[:, 128:256] + terms[:, 256:384] + terms[:, 384:512]
+
+    for step in range(NQ + 3):
+        if step < NQ:
+            zeta_part(step)
+            zeta_send(step)
+        if step == 0:
+            s_far(0)
+            s_far(1)
+        if 0 <= step - 1 < NQ:
+            zeta_done(step - 1)
+        if step == 2:
+            s_all()
+        if 0 <= step - 2 < NQ:
+            coupling_part(step - 2)
+        if 0 <= step - 3 < NQ:
+            coupling_done(step - 3)
+        if step == NQ:
+            for d in range(1, 8):
+                arrived(fa.at[lax.rem(r + 8 - d, 8)], fr_recv.at[d])
+            ca[c, 8:16] = jnp.sum(fa[...], axis=0)
+            ca[c, 0:8] = jnp.zeros((8, 128), F32)
 
     sums = jnp.sum(cross[...].T, axis=0, keepdims=True)
     for n in range(6):
@@ -376,12 +416,12 @@
 
     @pl.when(same)
     def _():
-        for copy in factor_copies(0) + [sigma_other()] + spread_copies():
+        for copy in factor_copies(0) + sigma_copy(1 - lax.rem(z, 2)) + spread_copies():
             copy.wait_send()
 
     @pl.when(other)
     def _():
-        for copy in factor_copies(1) + [sigma_copy(0), sigma_copy(1)]:
+        for copy in factor_copies(1) + sigma_copy(0) + sigma_copy(1):
             copy.wait_send()
 
     for copy in pending:
@@ -399,19 +439,19 @@
             jax.ShapeDtypeStruct((768, 512), F32),
             jax.ShapeDtypeStruct((1, 48), F32),
         ),
-        in_specs=[any_space, vmem, vmem, smem, smem, vmem],
+        in_specs=[any_space, vmem, vmem, vmem, smem, vmem],
         out_specs=(vmem, vmem),
         scratch_shapes=[
-            pltpu.VMEM((4, 2, 48, 768), BF16),
-            pltpu.VMEM((2, 4, 2, 2, 48, 768), BF16),
+            pltpu.VMEM((4, 96, 768), BF16),
+            pltpu.VMEM((2, 4, 2, 96, 768), BF16),
             pltpu.VMEM((2, 4, 2, 384, 512), BF16),
-            pltpu.VMEM((4, 4, 512, 512), BF16),
-            pltpu.VMEM((NQ, 4, 4, 48, 512), F32),
-            pltpu.VMEM((NQ, 3, 48, 2176), jnp.int16),
-            pltpu.VMEM((NQ, 3, 48, 2176), jnp.int16),
-            pltpu.VMEM((NQ, 4, 4, 48, 512), BF16),
-            pltpu.VMEM((NQ, 3, 192, 512), BF16),
-            pltpu.VMEM((NQ, 3, 192, 512), BF16),
+            pltpu.VMEM((4, 4, 2, 256, 512), BF16),
+            pltpu.VMEM((2, 4, 4, 96, 512), F32),
+            pltpu.VMEM((2, 3, 96, 2176), jnp.int16),
+            pltpu.VMEM((2, 3, 96, 2176), jnp.int16),
+            pltpu.VMEM((2, 4, 4, 96, 512), BF16),
+            pltpu.VMEM((2, 3, 4, 96, 512), BF16),
+            pltpu.VMEM((2, 3, 4, 96, 512), BF16),
             pltpu.VMEM((768, 128), F32),
             pltpu.VMEM((8, 128), F32),
             pltpu.VMEM((8, 8, 128), F32),
@@ -420,7 +460,7 @@
             dma((3,)),
             dma((4,)), dma((4, 2)), dma((4,)), dma((2,)),
             dma((6,)), dma((6,)), dma((4,)), dma((4,)),
-            dma((2,)), dma((2,)), dma((6,)), dma((6,)), dma((4,)), dma((4,)),
+            dma((2, 2)), dma((2, 2)), dma((2, 6)), dma((2, 6)), dma((2, 4)), dma((2, 4)),
             dma((NQ, 3)), dma((NQ, 3)), dma((NQ, 3)), dma((NQ, 3)), dma((NQ, 3)), dma((NQ, 3)),
             dma((8,)), dma((8,)),
             dma((8,)), dma((8,)), dma((16,)), dma((16,)),

time: 136 us -> 132 us (0.971)
  Pallas kernels: 131 us -> 126 us
    pallas_call x1, Pallas kernels: 131 us -> 126 us  [per_device(): pl.pallas_call(kernel, out_shape=(jax.ShapeDtypeStruct((768, 512), F32),...]
where the time goes in v3:
time: 132 us
  Pallas kernels  126 us (95%)
  local copies, waits for them, and re-layouts  4.54 us (3%)
    pallas_call x1, Pallas kernels, per_device(): pl.pallas_call(kernel, out_shape=(jax.ShapeDtypeStruct((768, 512), F32),...  126 us
    unnamed x5, local copies, waits for them, and re-layouts  4.54 us

profile of v3, /device:TPU:1, one launch (start us, length us, event | category | flops | bytes accessed | tf_op | source)
XLA Modules:
  0.0 131.6 jit_solution(7985121529729611152)
XLA Ops:
  0.6 1.4 %copy.8.pattern_ref = s32[16,4]{1,0:T(8,128)} copy(s32[16,4]{0,1:T(4,128)} %param.9) | data formatting | bytes 512 | tf_op args[3]
  2.0 126.4 %shard_map.77 = (f32[768,512]{1,0:T(8,128)}, f32[1,48]{1,0:T(1,128)}) custom-call(bf16[512,1024]{1,0:T(8,128)(2,1)} %sigma_ref.1, bf16[768,512]{1,0:T(8,128)(2,1)} %l_ref.1, bf16[768,384]{1,0:T(8,128)(2,1)} %g_ref.1, s32[16,4]{1,0:T(8,128)} %copy.8.pattern_ref, s32[16]{0:T(128)} %sizes_ref.1, s32[1,48]{1,0:T(1,128)} %bitcast.2), custom_call_target="tpu_custom_call" | custom-call | tf_op jit(solution)/shard_map/pallas_call | solution.py:436
  128.4 0.0 copy-start
  128.4 2.7 %copy.11 = f32[768,512]{1,0:T(8,128)} copy(f32[768,512]{1,0:T(8,128)} %get-tuple-element.8) | data formatting | bytes 3145728
  131.1 0.0 copy-done
  131.1 0.5 copy.12
Async XLA Ops:
  128.4 2.7 %copy-start = (f32[1,48]{1,0:T(1,128)S(1)}, f32[1,48]{1,0:T(1,128)}, u32[]{:S(2)}) copy-start(f32[1,48]{1,0:T(1,128)} %get-tuple-element.5) | copy-start | bytes 580

commit v4 on v3

--- a/solution.py
+++ b/solution.py
@@ -9,7 +9,18 @@
 MESH = pl.DeviceIdType.MESH
 F32 = jnp.float32
 BF16 = jnp.bfloat16
-CHUNKS = ((0, 0, 48), (0, 48, 48), (1, 0, 48), (1, 48, 32), (1, 80, 16))
+PASSES = ((0, 0, 32), (0, 32, 64), (1, 0, 96))
+PASS_PIECES = ((0, 1), (2, 3), (4, 5, 6, 7))
+PIECES = (
+    (0, 0, 16), (0, 16, 16), (0, 32, 32), (0, 64, 32),
+    (1, 0, 32), (1, 32, 32), (1, 64, 16), (1, 80, 16),
+)
+CHUNKS = ((0, 0, 32), (0, 32, 32), (0, 64, 32), (1, 0, 32), (1, 32, 32), (1, 64, 16), (1, 80, 16))
+CHUNK_PIECES = ((0, 1), (2,), (3,), (4,), (5,), (6,), (7,))
+ORDER = (
+    "d0 d1 d2 c0 d3 c1 f0 d4 c2 d5 f1 d6 c3 d7 f2 c4 c5 f3 c6 f4 f5 f6"
+).split()
+NP = len(PIECES)
 NQ = len(CHUNKS)
 FAR_ORDER = (2, 1, 3)
 
@@ -70,14 +81,16 @@
     for s in range(NSUP):
         total_size = total_size + sizes_ref[s]
         ends.append(total_size)
+    pattern = pattern_ref[...].astype(F32)
     block_mask = []
     for n in range(6):
         place = jnp.int32(0)
         for s in range(NSUP):
             place = place + (ends[s] <= 6 * r + n).astype(jnp.int32)
         place = jnp.minimum(place, NSUP - 1)
-        row = pattern_ref[pl.ds(place, 1), :].astype(F32)
-        block_mask.append([row[:, m:m + 1] for m in range(4)])
+        lane = lax.broadcasted_iota(jnp.int32, (4, NSUP), 1)
+        column = jnp.sum(jnp.where(lane == place, pattern, 0.0), axis=1, keepdims=True)
+        block_mask.append([column[m:m + 1] for m in range(4)])
 
     for n in range(6):
         for m in range(4):
@@ -235,12 +248,20 @@
         arrived(sbuf.at[y, 2 * i + s_block[1], h], sa_recv.at[s_block[1], h])
     s_first(1)
 
-    def spread_copies():
-        slot = gbuf.at[lax.rem(z, 2)]
-        return [
-            remote(slot, slot, gg_send.at[d], gg_recv.at[lax.rem(z, 2)], r, 4 * x + at_z(d))
-            for d in FAR_ORDER
-        ]
+    def g_half(zl, half):
+        return gbuf.at[zl, pl.ds(2 * half, 2)]
+
+    def g_copy(zl, half, n, d):
+        return remote(
+            g_half(zl, half), g_half(zl, half), gg_send.at[zl, n], gg_recv.at[zl, n],
+            r, 4 * x + at_z(d),
+        )
+
+    def g_source(zl):
+        return [g_copy(zl, 0, 0, 1), g_copy(zl, 1, 2, 3), g_copy(zl, 1, 1, 1), g_copy(zl, 0, 3, 3)]
+
+    def g_from(zl):
+        return lax.rem(z + 4 - (2 * i + zl), 4)
 
     @pl.when(same)
     def _():
@@ -250,10 +271,57 @@
                 if d or rel:
                     src_core = 1 - i if rel else i
                     arrived(gbuf.at[lax.rem(z, 2), at_x(4 - d), src_core], ga_recv.at[d, rel])
-        for copy in spread_copies():
-            copy.start()
+
+    for zl in range(2):
+        @pl.when(g_from(zl) == 0)
+        def _():
+            for copy in g_source(zl):
+                copy.start()
+
+    def g_forward():
+        for zl in range(2):
+            @pl.when(g_from(zl) == 1)
+            def _():
+                arrived(g_half(zl, 0), gg_recv.at[zl, 0])
+                g_copy(zl, 0, 4, 1).start()
+
+            @pl.when(g_from(zl) == 3)
+            def _():
+                arrived(g_half(zl, 1), gg_recv.at[zl, 2])
+                g_copy(zl, 1, 5, 3).start()
+
+    def g_rest():
+        for zl in range(2):
+            @pl.when(g_from(zl) == 1)
+            def _():
+                arrived(g_half(zl, 1), gg_recv.at[zl, 1])
+
+            @pl.when(g_from(zl) == 3)
+            def _():
+                arrived(g_half(zl, 0), gg_recv.at[zl, 3])
+
+            @pl.when(g_from(zl) == 2)
+            def _():
+                arrived(g_half(zl, 0), gg_recv.at[zl, 4])
+                arrived(g_half(zl, 1), gg_recv.at[zl, 5])
+
+    def g_sent():
+        for zl in range(2):
+            @pl.when(g_from(zl) == 0)
+            def _():
+                for copy in g_source(zl):
+                    copy.wait_send()
+
+            @pl.when(g_from(zl) == 1)
+            def _():
+                g_copy(zl, 0, 4, 1).wait_send()
+
+            @pl.when(g_from(zl) == 3)
+            def _():
+                g_copy(zl, 1, 5, 3).wait_send()
 
     s_forward(0)
+    g_forward()
     ring_forward(m_slot, m_send, m_recv, x_right, x_left, at_x)
     ring_rest(m_slot, m_recv, at_x)
     m_share(1, at_x(3))
@@ -264,15 +332,12 @@
 
     ring_far(m_slot, m_recv, at_x)
     m_share(3, at_x(2))
-    for zl in range(2):
-        @pl.when(z != 2 * i + zl)
-        def _():
-            arrived(gbuf.at[zl], gg_recv.at[zl])
+    g_rest()
     for n, d in enumerate((0, 3, 1, 2)):
         arrived(mbuf.at[1 - i, at_x(d)], m_sib_recv.at[n])
 
     def zeta_part(q):
-        zl, start, rows = CHUNKS[q]
+        zl, start, rows = PASSES[q]
         here = slice(start, start + rows)
         g0 = gbuf[zl, :, 0, here].reshape(4 * rows, 768)
         g1 = gbuf[zl, :, 1, here].reshape(4 * rows, 768)
@@ -286,7 +351,7 @@
         lax.fori_loop(0, 4, step, 0)
 
     def zeta_send(q):
-        zl, start, rows = CHUNKS[q]
+        zl, start, rows = PIECES[q]
         here = slice(start, start + rows)
         for d in FAR_ORDER:
             parts = [acc[zl, at_y(d), k, here] for k in range(4)]
@@ -308,7 +373,7 @@
             )
 
     def zeta_done(q):
-        zl, start, rows = CHUNKS[q]
+        zl, start, rows = PIECES[q]
         here = slice(start, start + rows)
         for d in range(3):
             arrived(yrecv.at[zl, d, pl.ds(start, rows)], y_recv.at[q, d])
@@ -344,8 +409,10 @@
     def coupling_part(q):
         zl, start, rows = CHUNKS[q]
         here = pl.ds(start, rows)
-        for d in range(1, 4):
-            arrived(zc.at[zl, :, at_x(4 - d), here], x_recv.at[q, d - 1])
+        for piece in CHUNK_PIECES[q]:
+            _, first, some = PIECES[piece]
+            for d in range(1, 4):
+                arrived(zc.at[zl, :, at_x(4 - d), pl.ds(first, some)], x_recv.at[piece, d - 1])
         for d in FAR_ORDER:
             pbuf[zl, d - 1, :, start:start + rows] = product(q, at_z(d)).astype(BF16).reshape(4, rows, 512)
             send(
@@ -369,26 +436,24 @@
             terms = total * zc[zl, x, p, start:start + rows].astype(F32)
             cross[place, :] = terms[:, 0:128] + terms[:, 128:256] + terms[:, 256:384] + terms[:, 384:512]
 
-    for step in range(NQ + 3):
-        if step < NQ:
-            zeta_part(step)
-            zeta_send(step)
-        if step == 0:
+    for n, pieces in enumerate(PASS_PIECES):
+        zeta_part(n)
+        for piece in pieces:
+            zeta_send(piece)
+        if n == 0:
             s_far(0)
+        if n == 1:
             s_far(1)
-        if 0 <= step - 1 < NQ:
-            zeta_done(step - 1)
-        if step == 2:
+    for item in ORDER:
+        n = int(item[1])
+        if item == "c0":
             s_all()
-        if 0 <= step - 2 < NQ:
-            coupling_part(step - 2)
-        if 0 <= step - 3 < NQ:
-            coupling_done(step - 3)
-        if step == NQ:
+        if item == "f4":
             for d in range(1, 8):
                 arrived(fa.at[lax.rem(r + 8 - d, 8)], fr_recv.at[d])
             ca[c, 8:16] = jnp.sum(fa[...], axis=0)
             ca[c, 0:8] = jnp.zeros((8, 128), F32)
+        {"d": zeta_done, "c": coupling_part, "f": coupling_done}[item[0]](n)
 
     sums = jnp.sum(cross[...].T, axis=0, keepdims=True)
     for n in range(6):
@@ -416,7 +481,7 @@
 
     @pl.when(same)
     def _():
-        for copy in factor_copies(0) + sigma_copy(1 - lax.rem(z, 2)) + spread_copies():
+        for copy in factor_copies(0) + sigma_copy(1 - lax.rem(z, 2)):
             copy.wait_send()
 
     @pl.when(other)
@@ -424,6 +489,7 @@
         for copy in factor_copies(1) + sigma_copy(0) + sigma_copy(1):
             copy.wait_send()
 
+    g_sent()
     for copy in pending:
         copy.wait_send()
 
@@ -458,17 +524,17 @@
             pltpu.VMEM((16, 16, 128), F32),
             pltpu.VMEM((8, 8, 128), F32),
             dma((3,)),
-            dma((4,)), dma((4, 2)), dma((4,)), dma((2,)),
+            dma((4,)), dma((4, 2)), dma((2, 6)), dma((2, 6)),
             dma((6,)), dma((6,)), dma((4,)), dma((4,)),
             dma((2, 2)), dma((2, 2)), dma((2, 6)), dma((2, 6)), dma((2, 4)), dma((2, 4)),
-            dma((NQ, 3)), dma((NQ, 3)), dma((NQ, 3)), dma((NQ, 3)), dma((NQ, 3)), dma((NQ, 3)),
+            dma((NP, 3)), dma((NP, 3)), dma((NP, 3)), dma((NP, 3)), dma((NQ, 3)), dma((NQ, 3)),
             dma((8,)), dma((8,)),
             dma((8,)), dma((8,)), dma((16,)), dma((16,)),
         ],
         compiler_params=pltpu.CompilerParams(
             collective_id=0, has_side_effects=True, vmem_limit_bytes=60 * 1024 * 1024
         ),
-    )(sigma_ss, l_cs, g_cc, pattern, sup_sizes, owner.reshape(1, 48))
+    )(sigma_ss, l_cs, g_cc, pattern.T, sup_sizes, owner.reshape(1, 48))
     return (sel_cs, log_var.reshape(48))
 
 

time: 132 us -> 125 us (0.947)
  Pallas kernels: 126 us -> 121 us
  local copies, waits for them, and re-layouts: 4.54 us -> 3.19 us
    pallas_call x1, Pallas kernels: 126 us -> 121 us  [per_device(): pl.pallas_call(kernel, out_shape=(jax.ShapeDtypeStruct((768, 512), F32),...]
    unnamed x5 -> x4, local copies, waits for them, and re-layouts: 4.54 us -> 3.19 us
where the time goes in v4:
time: 125 us
  Pallas kernels  121 us (97%)
  local copies, waits for them, and re-layouts  3.19 us (3%)
    pallas_call x1, Pallas kernels, per_device(): pl.pallas_call(kernel, out_shape=(jax.ShapeDtypeStruct((768, 512), F32),...  121 us
    unnamed x4, local copies, waits for them, and re-layouts  3.19 us

profile of v4, /device:TPU:1, one launch (start us, length us, event | category | flops | bytes accessed | tf_op | source)
XLA Modules:
  0.0 124.7 jit_solution(11967729790575447361)
XLA Ops:
  0.6 120.8 %shard_map.77 = (f32[768,512]{1,0:T(8,128)}, f32[1,48]{1,0:T(1,128)}) custom-call(bf16[512,1024]{1,0:T(8,128)(2,1)} %sigma_ref.1, bf16[768,512]{1,0:T(8,128)(2,1)} %l_ref.1, bf16[768,384]{1,0:T(8,128)(2,1)} %g_ref.1, s32[4,16]{1,0:T(4,128)} %bitcast.3, s32[16]{0:T(128)} %sizes_ref.1, s32[1,48]{1,0:T(1,128)} %bitcast.4), custom_call_target="tpu_custom_call" | custom-call | tf_op jit(solution)/shard_map/pallas_call | solution.py:502
  121.5 0.0 copy-start
  121.5 2.7 %copy.10 = f32[768,512]{1,0:T(8,128)} copy(f32[768,512]{1,0:T(8,128)} %get-tuple-element.8) | data formatting | bytes 3145728
  124.1 0.0 copy-done
  124.2 0.5 copy.11
Async XLA Ops:
  121.5 2.7 %copy-start = (f32[1,48]{1,0:T(1,128)S(1)}, f32[1,48]{1,0:T(1,128)}, u32[]{:S(2)}) copy-start(f32[1,48]{1,0:T(1,128)} %get-tuple-element.5) | copy-start | bytes 580

commit v5 on v4

--- a/solution.py
+++ b/solution.py
@@ -10,26 +10,28 @@
 F32 = jnp.float32
 BF16 = jnp.bfloat16
 PASSES = ((0, 0, 32), (0, 32, 64), (1, 0, 96))
-PASS_PIECES = ((0, 1), (2, 3), (4, 5, 6, 7))
+PASS_PIECES = ((0,), (1, 2), (3, 4, 5, 6))
 PIECES = (
-    (0, 0, 16), (0, 16, 16), (0, 32, 32), (0, 64, 32),
+    (0, 0, 32), (0, 32, 32), (0, 64, 32),
     (1, 0, 32), (1, 32, 32), (1, 64, 16), (1, 80, 16),
 )
 CHUNKS = ((0, 0, 32), (0, 32, 32), (0, 64, 32), (1, 0, 32), (1, 32, 32), (1, 64, 16), (1, 80, 16))
-CHUNK_PIECES = ((0, 1), (2,), (3,), (4,), (5,), (6,), (7,))
+CHUNK_PIECES = ((0,), (1,), (2,), (3,), (4,), (5,), (6,))
 ORDER = (
-    "d0 d1 d2 c0 d3 c1 f0 d4 c2 d5 f1 d6 c3 d7 f2 c4 c5 f3 c6 f4 f5 f6"
-).split()
+    ("d", 0), ("d", 1), ("c", 0), ("d", 2), ("c", 1), ("f", 0), ("d", 3), ("c", 2), ("d", 4),
+    ("f", 1), ("d", 5), ("c", 3), ("d", 6), ("f", 2), ("c", 4), ("c", 5), ("f", 3), ("c", 6), ("f", 4),
+    ("f", 5), ("f", 6),
+)
 NP = len(PIECES)
 NQ = len(CHUNKS)
 FAR_ORDER = (2, 1, 3)
 
 
 def kernel(
-    sigma_ref, l_ref, g_ref, pattern_ref, sizes_ref, owner_ref,
-    out_ref, log_ref,
-    gt_ref, gbuf, mbuf, sbuf, acc, ysend, yrecv, zc, pbuf, rz, cross, fac_ref, fa, ca, cb,
-    local_sem, ga_send, ga_recv, gg_send, gg_recv,
+    sigma_ref, l_hbm, g_hbm, pattern_ref, sizes_ref, owner_ref,
+    sel_ref, log_ref,
+    out_ref, l_ref, g_ref, gt_ref, gbuf, mbuf, sbuf, acc, ysend, yrecv, zc, pbuf, rz, cross, fac_ref, fa, ca, cb,
+    local_sem, out_sem, ga_send, ga_recv, gg_send, gg_recv,
     m_send, m_recv, m_sib_send, m_sib_recv,
     sa_send, sa_recv, s_send, s_recv, s_sib_send, s_sib_recv,
     y_send, y_recv, x_send, x_recv, z_send, z_recv,
@@ -69,6 +71,11 @@
         copy.start()
         pending.append(copy)
 
+    def sent():
+        for copy in pending:
+            copy.wait_send()
+        pending.clear()
+
     barrier = pltpu.get_barrier_semaphore()
     partners = [(r, lax.rem(c + d, 16)) for d in range(1, 16)]
     partners += [(lax.rem(r + d, 8), c) for d in range(1, 8)]
@@ -76,6 +83,10 @@
     partners += [(sib, 4 * x + at_z(d)) for d in range(1, 4)]
     for partner in partners:
         pl.semaphore_signal(barrier, inc=1, device_id=partner, device_id_type=MESH)
+    l_copy = pltpu.make_async_copy(l_hbm, l_ref, local_sem.at[3])
+    g_copy_in = pltpu.make_async_copy(g_hbm, g_ref, local_sem.at[4])
+    g_copy_in.start()
+    l_copy.start()
 
     ends, total_size = [], jnp.int32(0)
     for s in range(NSUP):
@@ -92,19 +103,21 @@
         column = jnp.sum(jnp.where(lane == place, pattern, 0.0), axis=1, keepdims=True)
         block_mask.append([column[m:m + 1] for m in range(4)])
 
+    g_copy_in.wait()
+    gt_ref[...] = g_ref[...].T.reshape(4, 96, 768)
+    wide = g_ref[...].astype(F32)
+    squares = jnp.sum(wide * wide, axis=0, keepdims=True)
+    fac_ref[...] = jnp.zeros((8, 128), F32)
+    for n in range(3):
+        fac_ref[n:n + 1] = squares[:, n * 128:(n + 1) * 128]
+
+    l_copy.wait()
     for n in range(6):
         for m in range(4):
             block = l_ref[n * 128:(n + 1) * 128, m * 128:(m + 1) * 128].astype(F32)
             mbuf[i, x, n // 3, (n % 3) * 128:(n % 3 + 1) * 128, m * 128:(m + 1) * 128] = (
                 block * block_mask[n][m]
             ).astype(BF16)
-    gt_ref[...] = g_ref[...].T.reshape(4, 96, 768)
-    wide = g_ref[...].astype(F32)
-    squares = jnp.sum(wide * wide, axis=0, keepdims=True)
-    fac_ref[...] = jnp.zeros((8, 128), F32)
-    for n in range(3):
-        fac_ref[n:n + 1] = squares[:, n * 128:(n + 1) * 128]
-
     pl.semaphore_wait(barrier, len(partners))
 
     fa[r] = fac_ref[...]
@@ -423,6 +436,10 @@
         for place, part in row_places(q):
             out_ref[place, :] = total[part]
 
+    def out_copy(q, p):
+        place = row_places(q)[p][0]
+        return pltpu.make_async_copy(out_ref.at[place], sel_ref.at[place], out_sem.at[q, p])
+
     def coupling_done(q):
         zl, start, rows = CHUNKS[q]
         for d in range(3):
@@ -432,7 +449,11 @@
             for d in range(3):
                 total += rz[zl, d, p, start:start + rows].astype(F32)
             total = -total
-            out_ref[place, :] = total
+            block = (zl * 384 + p * 96 + start) // 128
+            out_ref[place, :] = jnp.concatenate(
+                [total[:, m * 128:(m + 1) * 128] * block_mask[block][m] for m in range(4)], axis=1
+            )
+            out_copy(q, p).start()
             terms = total * zc[zl, x, p, start:start + rows].astype(F32)
             cross[place, :] = terms[:, 0:128] + terms[:, 128:256] + terms[:, 256:384] + terms[:, 384:512]
 
@@ -444,26 +465,36 @@
             s_far(0)
         if n == 1:
             s_far(1)
-    for item in ORDER:
-        n = int(item[1])
-        if item == "c0":
+    for kind, n in ORDER:
+        if (kind, n) == ("c", 0):
             s_all()
-        if item == "f4":
+        if (kind, n) == ("f", 4):
             for d in range(1, 8):
                 arrived(fa.at[lax.rem(r + 8 - d, 8)], fr_recv.at[d])
             ca[c, 8:16] = jnp.sum(fa[...], axis=0)
             ca[c, 0:8] = jnp.zeros((8, 128), F32)
-        {"d": zeta_done, "c": coupling_part, "f": coupling_done}[item[0]](n)
+        {"d": zeta_done, "c": coupling_part, "f": coupling_done}[kind](n)
 
     sums = jnp.sum(cross[...].T, axis=0, keepdims=True)
     for n in range(6):
         ca[c, n:n + 1] = sums[:, n * 128:(n + 1) * 128]
     for d in range(1, 16):
         send(ca.at[c], ca.at[c], cc_send.at[d], cc_recv.at[d], r, lax.rem(c + d, 16))
-    for n in range(6):
-        for m in range(4):
-            rows, columns = slice(n * 128, (n + 1) * 128), slice(m * 128, (m + 1) * 128)
-            out_ref[rows, columns] = out_ref[rows, columns] * block_mask[n][m]
+    @pl.when(same)
+    def _():
+        for copy in factor_copies(0) + sigma_copy(1 - lax.rem(z, 2)):
+            copy.wait_send()
+
+    @pl.when(other)
+    def _():
+        for copy in factor_copies(1) + sigma_copy(0) + sigma_copy(1):
+            copy.wait_send()
+
+    g_sent()
+    sent()
+    for q in range(NQ):
+        for p in range(4):
+            out_copy(q, p).wait()
     for d in range(1, 16):
         arrived(ca.at[lax.rem(c + 16 - d, 16)], cc_recv.at[d])
     cb[r] = jnp.sum(ca[:, 0:8], axis=0)
@@ -479,19 +510,12 @@
         picked = jnp.where(wanted - float(128 * n) == lanes, row, picked)
     log_ref[...] = jnp.sum(picked.T, axis=0, keepdims=True)
 
-    @pl.when(same)
-    def _():
-        for copy in factor_copies(0) + sigma_copy(1 - lax.rem(z, 2)):
-            copy.wait_send()
-
-    @pl.when(other)
-    def _():
-        for copy in factor_copies(1) + sigma_copy(0) + sigma_copy(1):
-            copy.wait_send()
-
-    g_sent()
-    for copy in pending:
-        copy.wait_send()
+    sent()
+
+
+def hand_over(from_ref, log_from_ref, to_ref, log_to_ref):
+    to_ref[...] = from_ref[...]
+    log_to_ref[...] = log_from_ref[...]
 
 
 def per_device(sigma_ss, l_cs, g_cc, pattern, sup_sizes, owner):
@@ -505,9 +529,12 @@
             jax.ShapeDtypeStruct((768, 512), F32),
             jax.ShapeDtypeStruct((1, 48), F32),
         ),
-        in_specs=[any_space, vmem, vmem, vmem, smem, vmem],
-        out_specs=(vmem, vmem),
+        in_specs=[any_space, any_space, any_space, vmem, smem, vmem],
+        out_specs=(any_space, vmem),
         scratch_shapes=[
+            pltpu.VMEM((768, 512), F32),
+            pltpu.VMEM((768, 512), BF16),
+            pltpu.VMEM((768, 384), BF16),
             pltpu.VMEM((4, 96, 768), BF16),
             pltpu.VMEM((2, 4, 2, 96, 768), BF16),
             pltpu.VMEM((2, 4, 2, 384, 512), BF16),
@@ -523,7 +550,7 @@
             pltpu.VMEM((8, 8, 128), F32),
             pltpu.VMEM((16, 16, 128), F32),
             pltpu.VMEM((8, 8, 128), F32),
-            dma((3,)),
+            dma((5,)), dma((NQ, 4)),
             dma((4,)), dma((4, 2)), dma((2, 6)), dma((2, 6)),
             dma((6,)), dma((6,)), dma((4,)), dma((4,)),
             dma((2, 2)), dma((2, 2)), dma((2, 6)), dma((2, 6)), dma((2, 4)), dma((2, 4)),
@@ -535,6 +562,12 @@
             collective_id=0, has_side_effects=True, vmem_limit_bytes=60 * 1024 * 1024
         ),
     )(sigma_ss, l_cs, g_cc, pattern.T, sup_sizes, owner.reshape(1, 48))
+    sel_cs, log_var = pl.pallas_call(
+        hand_over,
+        out_shape=(jax.ShapeDtypeStruct((768, 512), F32), jax.ShapeDtypeStruct((1, 48), F32)),
+        in_specs=[vmem, vmem],
+        out_specs=(vmem, vmem),
+    )(sel_cs, log_var)
     return (sel_cs, log_var.reshape(48))
 
 

time: 125 us -> 123 us (0.984)
  local copies, waits for them, and re-layouts: 3.19 us -> 0 us
    unnamed x4 -> x0, local copies, waits for them, and re-layouts: 3.19 us -> none
    pallas_call x0 -> x1, Pallas kernels: none -> 2.66 us  [per_device(): pl.pallas_call(hand_over, out_shape=(jax.ShapeDtypeStruct((768, 512), F32...]
where the time goes in v5:
time: 123 us
  Pallas kernels  122 us (99%)
    pallas_call x1, Pallas kernels, per_device(): pl.pallas_call(kernel, out_shape=(jax.ShapeDtypeStruct((768, 512), F32),...  120 us
    pallas_call x1, Pallas kernels, per_device(): pl.pallas_call(hand_over, out_shape=(jax.ShapeDtypeStruct((768, 512), F32...  2.66 us

profile of v5, /device:TPU:1, one launch (start us, length us, event | category | flops | bytes accessed | tf_op | source)
XLA Modules:
  0.0 123.0 jit_solution(14805287050600683381)
XLA Ops:
  0.6 119.7 %shard_map.77 = (f32[768,512]{1,0:T(8,128)}, f32[1,48]{1,0:T(1,128)}) custom-call(bf16[512,1024]{1,0:T(8,128)(2,1)} %sigma_ref.1, bf16[768,512]{1,0:T(8,128)(2,1)} %l_hbm.1, bf16[768,384]{1,0:T(8,128)(2,1)} %g_hbm.1, s32[4,16]{1,0:T(4,128)} %bitcast.3, s32[16]{0:T(128)} %sizes_ref.1, s32[1,48]{1,0:T(1,128)} %bitcast.4), custom_call_target="tpu_custom_call" | custom-call | tf_op jit(solution)/shard_map/pallas_call | solution.py:526
  120.3 2.7 %shard_map.78 = (f32[768,512]{1,0:T(8,128)}, f32[1,48]{1,0:T(1,128)}) custom-call(f32[768,512]{1,0:T(8,128)} %get-tuple-element.6.from_ref, f32[1,48]{1,0:T(1,128)} %get-tuple-element.7.log_from_ref), custom_call_target="tpu_custom_call" | custom-call | tf_op jit(solution)/shard_map/pallas_call | solution.py:565

commit v6 on v5

--- a/solution.py
+++ b/solution.py
@@ -18,9 +18,7 @@
 CHUNKS = ((0, 0, 32), (0, 32, 32), (0, 64, 32), (1, 0, 32), (1, 32, 32), (1, 64, 16), (1, 80, 16))
 CHUNK_PIECES = ((0,), (1,), (2,), (3,), (4,), (5,), (6,))
 ORDER = (
-    ("d", 0), ("d", 1), ("c", 0), ("d", 2), ("c", 1), ("f", 0), ("d", 3), ("c", 2), ("d", 4),
-    ("f", 1), ("d", 5), ("c", 3), ("d", 6), ("f", 2), ("c", 4), ("c", 5), ("f", 3), ("c", 6), ("f", 4),
-    ("f", 5), ("f", 6),
+    ("d", 0), ("d", 1), ("c", 0), ("d", 2), ("c", 1), ("d", 3), ("f", 0), ("c", 2), ("d", 4), ("d", 5), ("f", 1), ("c", 3), ("d", 6), ("f", 2), ("c", 4), ("c", 5), ("f", 3), ("c", 6), ("f", 4), ("f", 5), ("f", 6),
 )
 NP = len(PIECES)
 NQ = len(CHUNKS)
@@ -257,10 +255,6 @@
 
     s_first(0)
 
-    for h in range(2):
-        arrived(sbuf.at[y, 2 * i + s_block[1], h], sa_recv.at[s_block[1], h])
-    s_first(1)
-
     def g_half(zl, half):
         return gbuf.at[zl, pl.ds(2 * half, 2)]
 
@@ -290,6 +284,10 @@
         def _():
             for copy in g_source(zl):
                 copy.start()
+
+    for h in range(2):
+        arrived(sbuf.at[y, 2 * i + s_block[1], h], sa_recv.at[s_block[1], h])
+    s_first(1)
 
     def g_forward():
         for zl in range(2):

time: 123 us -> 123 us (level)
  no operation moved by 1% of the time
where the time goes in v6:
time: 123 us
  Pallas kernels  122 us (99%)
    pallas_call x1, Pallas kernels, per_device(): pl.pallas_call(kernel, out_shape=(jax.ShapeDtypeStruct((768, 512), F32),...  119 us
    pallas_call x1, Pallas kernels, per_device(): pl.pallas_call(hand_over, out_shape=(jax.ShapeDtypeStruct((768, 512), F32...  2.66 us

profile of v6, /device:TPU:1, one launch (start us, length us, event | category | flops | bytes accessed | tf_op | source)
XLA Modules:
  0.0 122.5 jit_solution(7377312800946415174)
XLA Ops:
  0.6 119.2 %shard_map.77 = (f32[768,512]{1,0:T(8,128)}, f32[1,48]{1,0:T(1,128)}) custom-call(bf16[512,1024]{1,0:T(8,128)(2,1)} %sigma_ref.1, bf16[768,512]{1,0:T(8,128)(2,1)} %l_hbm.1, bf16[768,384]{1,0:T(8,128)(2,1)} %g_hbm.1, s32[4,16]{1,0:T(4,128)} %bitcast.3, s32[16]{0:T(128)} %sizes_ref.1, s32[1,48]{1,0:T(1,128)} %bitcast.4), custom_call_target="tpu_custom_call" | custom-call | tf_op jit(solution)/shard_map/pallas_call | solution.py:524
  119.9 2.7 %shard_map.78 = (f32[768,512]{1,0:T(8,128)}, f32[1,48]{1,0:T(1,128)}) custom-call(f32[768,512]{1,0:T(8,128)} %get-tuple-element.6.from_ref, f32[1,48]{1,0:T(1,128)} %get-tuple-element.7.log_from_ref), custom_call_target="tpu_custom_call" | custom-call | tf_op jit(solution)/shard_map/pallas_call | solution.py:563
